TPU v7x, 32 devices: a whole 2x2x4 slice. The times are simulated.
32 devices in a mesh: dp: 4 (over y, x), fsdp: 8 (over z, core).
Axes of the slice: x: 2, y: 2, z: 4, core: 2. Of those that a mesh axis runs over, the one named last changes fastest.
Arguments:
- tokens: bfloat16 [4096, 768], P(('dp', 'fsdp')), may hold values from -24 to 24
- lengths: int32 [32], P(('dp', 'fsdp')), may hold values from 1 to 128, 2560 in all
- cotangent: float32 [4096, 768], P(('dp', 'fsdp')), may hold values from -6 to 6
- query_weight: bfloat16 [768, 768], P(('dp', 'fsdp')), may hold values from -0.21875 to 0.21875
- query_bias: bfloat16 [768], P(('dp', 'fsdp')), may hold values from -3 to 3
- key_weight: bfloat16 [768, 768], P(('dp', 'fsdp')), may hold values from -0.21875 to 0.21875
- value_weight: bfloat16 [768, 768], P(('dp', 'fsdp')), may hold values from -0.21875 to 0.21875
- value_bias: bfloat16 [768], P(('dp', 'fsdp')), may hold values from -3 to 3
- out_weight: bfloat16 [768, 768], P(('dp', 'fsdp')), may hold values from -0.875 to 0.875
- out_bias: bfloat16 [768], P(('dp', 'fsdp')), may hold values from -3 to 3
- norm1_gain: bfloat16 [768], P(('dp', 'fsdp')), may hold values from 0.5 to 1.5
- norm1_shift: bfloat16 [768], P(('dp', 'fsdp')), may hold values from -3 to 3
- inner_weight: bfloat16 [768, 3072], P(('dp', 'fsdp')), may hold values from -0.21875 to 0.21875
- inner_bias: bfloat16 [3072], P(('dp', 'fsdp')), may hold values from -3 to 3
- outer_weight: bfloat16 [3072, 768], P(('dp', 'fsdp')), may hold values from -0.109375 to 0.109375
- outer_bias: bfloat16 [768], P(('dp', 'fsdp')), may hold values from -3 to 3
- norm2_gain: bfloat16 [768], P(('dp', 'fsdp')), may hold values from 0.5 to 1.5
- norm2_shift: bfloat16 [768], P(('dp', 'fsdp')), may hold values from -3 to 3
Outputs:
- layer_out: float32 [4096, 768], P(('dp', 'fsdp'))
- grad_tokens: float32 [4096, 768], P(('dp', 'fsdp'))
- grad_query_weight: float32 [768, 768], P(('dp', 'fsdp'))
- grad_query_bias: float32 [768], P(('dp', 'fsdp'))
- grad_key_weight: float32 [768, 768], P(('dp', 'fsdp'))
- grad_value_weight: float32 [768, 768], P(('dp', 'fsdp'))
- grad_value_bias: float32 [768], P(('dp', 'fsdp'))
- grad_out_weight: float32 [768, 768], P(('dp', 'fsdp'))
- grad_out_bias: float32 [768], P(('dp', 'fsdp'))
- grad_norm1_gain: float32 [768], P(('dp', 'fsdp'))
- grad_norm1_shift: float32 [768], P(('dp', 'fsdp'))
- grad_inner_weight: float32 [768, 3072], P(('dp', 'fsdp'))
- grad_inner_bias: float32 [3072], P(('dp', 'fsdp'))
- grad_outer_weight: float32 [3072, 768], P(('dp', 'fsdp'))
- grad_outer_bias: float32 [768], P(('dp', 'fsdp'))
- grad_norm2_gain: float32 [768], P(('dp', 'fsdp'))
- grad_norm2_shift: float32 [768], P(('dp', 'fsdp'))
Inputs may be any that keep to these rules, and one draw needn't show every extreme that they name: lengths sum to 2560 and the longest is exactly 128.
All inputs are finite; a program needn't handle non-finite values. No bound on the sum of `lengths` on one device may be relied on, other than what follows from the above.
Results may differ from a plain program's by a relative error of at most 0.013.
Values may be sent and summed in bfloat16 or wider, within the bound.
A program may use at most 192 MiB of HBM per device.

v0:
```python
import jax
import jax.numpy as jnp
from jax import lax
from jax.sharding import PartitionSpec as P

D = 768
HEADS = 12
HEAD_DIM = 64
FF = 3072


NORM_EPS = 1e-12
ATTN_SCALE = 0.125


def layer_norm(summed, gain, shift):
    center = summed - jnp.mean(summed, -1, keepdims=True)
    rstd = lax.rsqrt(jnp.mean(center * center, -1, keepdims=True) + NORM_EPS)
    normed = center * rstd
    return (normed * gain.astype(jnp.float32) + shift.astype(jnp.float32), normed, rstd)


def norm_back(grad_in, normed, rstd, gain):
    scaled = grad_in * gain.astype(jnp.float32)
    return rstd * (
        scaled
        - jnp.mean(scaled, -1, keepdims=True)
        - normed * jnp.mean(scaled * normed, -1, keepdims=True)
    )


def gelu_parts(pre):
    cdf = 0.5 * (1.0 + jax.scipy.special.erf(pre * 0.7071067811865476))
    slope = cdf + pre * jnp.exp(-0.5 * pre * pre) * 0.3989422804014327
    return (pre * cdf, slope)


def heads_of(rows):
    return rows.reshape(rows.shape[0], HEADS, HEAD_DIM)


def get_scores(query, keys, length):
    scores = (
        jnp.einsum(
            "qhd,khd->hqk", heads_of(query), heads_of(keys), preferred_element_type=jnp.float32
        )
        * ATTN_SCALE
    )
    valid = jnp.arange(scores.shape[-1]) < length
    return jnp.where(valid[None, None, :], scores, -1e30)


def forward_pass(tokens, length, weights):
    (
        query_weight,
        query_bias,
        key_weight,
        value_weight,
        value_bias,
        out_weight,
        out_bias,
        norm1_gain,
        norm1_shift,
        inner_weight,
        inner_bias,
        outer_weight,
        outer_bias,
        norm2_gain,
        norm2_shift,
    ) = weights
    f32 = jnp.float32
    bf16 = jnp.bfloat16
    query = (
        jnp.dot(tokens, query_weight, preferred_element_type=f32) + query_bias.astype(f32)
    ).astype(bf16)
    keys = jnp.dot(tokens, key_weight, preferred_element_type=f32).astype(bf16)
    values = (
        jnp.dot(tokens, value_weight, preferred_element_type=f32) + value_bias.astype(f32)
    ).astype(bf16)
    scores = get_scores(query, keys, length)
    top = jnp.max(scores, -1)
    lse = top + jnp.log(jnp.sum(jnp.exp(scores - top[..., None]), -1))
    probs_b = jnp.exp(scores - lse[..., None]).astype(bf16)
    mixed = jnp.einsum("hqk,khd->qhd", probs_b, heads_of(values), preferred_element_type=f32)
    mixed = mixed.reshape(tokens.shape[0], -1).astype(bf16)
    first_sum = (
        tokens.astype(f32)
        + jnp.dot(mixed, out_weight, preferred_element_type=f32)
        + out_bias.astype(f32)
    )
    hidden, normed_one, rstd_one = layer_norm(first_sum, norm1_gain, norm1_shift)
    hidden_b = hidden.astype(bf16)
    pre = jnp.dot(hidden_b, inner_weight, preferred_element_type=f32) + inner_bias.astype(f32)
    act, slope = gelu_parts(pre)
    act_b = act.astype(bf16)
    second_sum = (
        hidden + jnp.dot(act_b, outer_weight, preferred_element_type=f32) + outer_bias.astype(f32)
    )
    layer_out, normed_two, rstd_two = layer_norm(second_sum, norm2_gain, norm2_shift)
    saved = (
        query,
        keys,
        values,
        lse,
        mixed,
        normed_one,
        rstd_one,
        hidden_b,
        slope,
        act_b,
        normed_two,
        rstd_two,
    )
    return (layer_out, saved)


def backward_pass(tokens, cotangent, length, weights, saved):
    (
        query_weight,
        query_bias,
        key_weight,
        value_weight,
        value_bias,
        out_weight,
        out_bias,
        norm1_gain,
        norm1_shift,
        inner_weight,
        inner_bias,
        outer_weight,
        outer_bias,
        norm2_gain,
        norm2_shift,
    ) = weights
    (
        query,
        keys,
        values,
        lse,
        mixed,
        normed_one,
        rstd_one,
        hidden_b,
        slope,
        act_b,
        normed_two,
        rstd_two,
    ) = saved
    f32 = jnp.float32
    bf16 = jnp.bfloat16
    d_second = norm_back(cotangent, normed_two, rstd_two, norm2_gain)
    d_second_b = d_second.astype(bf16)
    d_pre = jnp.dot(d_second_b, outer_weight.T, preferred_element_type=f32) * slope
    d_pre_b = d_pre.astype(bf16)
    d_hidden = d_second + jnp.dot(d_pre_b, inner_weight.T, preferred_element_type=f32)
    d_first = norm_back(d_hidden, normed_one, rstd_one, norm1_gain)
    d_first_b = d_first.astype(bf16)
    d_mixed = jnp.dot(d_first_b, out_weight.T, preferred_element_type=f32).astype(bf16)
    again = jnp.exp(get_scores(query, keys, length) - lse[..., None])
    again_b = again.astype(bf16)
    d_probs = jnp.einsum(
        "qhd,khd->hqk", heads_of(d_mixed), heads_of(values), preferred_element_type=f32
    )
    d_values_f = jnp.einsum(
        "hqk,qhd->khd", again_b, heads_of(d_mixed), preferred_element_type=f32
    ).reshape(tokens.shape[0], -1)
    delta = jnp.sum(again * d_probs, -1, keepdims=True)
    d_scores = (again * (d_probs - delta) * ATTN_SCALE).astype(bf16)
    d_query_f = jnp.einsum(
        "hqk,khd->qhd", d_scores, heads_of(keys), preferred_element_type=f32
    ).reshape(tokens.shape[0], -1)
    d_keys_f = jnp.einsum(
        "hqk,qhd->khd", d_scores, heads_of(query), preferred_element_type=f32
    ).reshape(tokens.shape[0], -1)
    d_query = d_query_f.astype(bf16)
    d_keys = d_keys_f.astype(bf16)
    d_values = d_values_f.astype(bf16)
    grad_tokens = (
        d_first
        + jnp.dot(d_query, query_weight.T, preferred_element_type=f32)
        + jnp.dot(d_keys, key_weight.T, preferred_element_type=f32)
        + jnp.dot(d_values, value_weight.T, preferred_element_type=f32)
    )
    small = (
        jnp.sum(d_query_f, 0),
        jnp.sum(d_values_f, 0),
        jnp.sum(d_first, 0),
        jnp.sum(d_hidden * normed_one, 0),
        jnp.sum(d_hidden, 0),
        jnp.sum(d_pre, 0),
        jnp.sum(d_second, 0),
        jnp.sum(cotangent * normed_two, 0),
        jnp.sum(cotangent, 0),
    )
    factors = (
        tokens,
        d_query,
        d_keys,
        d_values,
        mixed,
        d_first_b,
        hidden_b,
        d_pre_b,
        act_b,
        d_second_b,
    )
    return (grad_tokens, small, factors)


def shards(
    tokens,
    lengths,
    cotangent,
    query_weight,
    query_bias,
    key_weight,
    value_weight,
    value_bias,
    out_weight,
    out_bias,
    norm1_gain,
    norm1_shift,
    inner_weight,
    inner_bias,
    outer_weight,
    outer_bias,
    norm2_gain,
    norm2_shift,
):
    length = lengths[0]
    whole = (
        lax.all_gather(query_weight, ("dp", "fsdp"), axis=0, tiled=True),
        lax.all_gather(query_bias, ("dp", "fsdp"), axis=0, tiled=True),
        lax.all_gather(key_weight, ("dp", "fsdp"), axis=0, tiled=True),
        lax.all_gather(value_weight, ("dp", "fsdp"), axis=0, tiled=True),
        lax.all_gather(value_bias, ("dp", "fsdp"), axis=0, tiled=True),
        lax.all_gather(out_weight, ("dp", "fsdp"), axis=0, tiled=True),
        lax.all_gather(out_bias, ("dp", "fsdp"), axis=0, tiled=True),
        lax.all_gather(norm1_gain, ("dp", "fsdp"), axis=0, tiled=True),
        lax.all_gather(norm1_shift, ("dp", "fsdp"), axis=0, tiled=True),
        lax.all_gather(inner_weight, ("dp", "fsdp"), axis=0, tiled=True),
        lax.all_gather(inner_bias, ("dp", "fsdp"), axis=0, tiled=True),
        lax.all_gather(outer_weight, ("dp", "fsdp"), axis=0, tiled=True),
        lax.all_gather(outer_bias, ("dp", "fsdp"), axis=0, tiled=True),
        lax.all_gather(norm2_gain, ("dp", "fsdp"), axis=0, tiled=True),
        lax.all_gather(norm2_shift, ("dp", "fsdp"), axis=0, tiled=True),
    )
    layer_out, saved = forward_pass(tokens, length, whole)
    weights_back = (
        lax.all_gather(query_weight, ("dp", "fsdp"), axis=0, tiled=True),
        lax.all_gather(query_bias, ("dp", "fsdp"), axis=0, tiled=True),
        lax.all_gather(key_weight, ("dp", "fsdp"), axis=0, tiled=True),
        lax.all_gather(value_weight, ("dp", "fsdp"), axis=0, tiled=True),
        lax.all_gather(value_bias, ("dp", "fsdp"), axis=0, tiled=True),
        lax.all_gather(out_weight, ("dp", "fsdp"), axis=0, tiled=True),
        lax.all_gather(out_bias, ("dp", "fsdp"), axis=0, tiled=True),
        lax.all_gather(norm1_gain, ("dp", "fsdp"), axis=0, tiled=True),
        lax.all_gather(norm1_shift, ("dp", "fsdp"), axis=0, tiled=True),
        lax.all_gather(inner_weight, ("dp", "fsdp"), axis=0, tiled=True),
        lax.all_gather(inner_bias, ("dp", "fsdp"), axis=0, tiled=True),
        lax.all_gather(outer_weight, ("dp", "fsdp"), axis=0, tiled=True),
        lax.all_gather(outer_bias, ("dp", "fsdp"), axis=0, tiled=True),
        lax.all_gather(norm2_gain, ("dp", "fsdp"), axis=0, tiled=True),
        lax.all_gather(norm2_shift, ("dp", "fsdp"), axis=0, tiled=True),
    )
    grad_tokens, small, factors = backward_pass(tokens, cotangent, length, weights_back, saved)
    tok_rows, d_query, d_keys, d_values, mixed, d_first_b, hidden_b, d_pre_b, act_b, d_second_b = (
        factors
    )
    devices = lax.axis_size("dp") * lax.axis_size("fsdp")
    total_rows = tokens.shape[0] * devices
    factor = 1.0 / jnp.sqrt(jnp.float32(total_rows))
    share = D // devices
    outer_share = FF // devices
    inner_rows = share * FF // D
    per_dev = 4 * share + inner_rows + outer_share

    def weight_block(left, right):
        return jnp.dot(left.T, right, preferred_element_type=jnp.float32)

    small_terms = tuple((g * factor for g in small))
    count_dev = per_dev * lax.axis_size(("dp", "fsdp")) // per_dev
    pieces = [
        weight_block(tok_rows, d_query).reshape(count_dev, share, D),
        weight_block(tok_rows, d_keys).reshape(count_dev, share, D),
        weight_block(tok_rows, d_values).reshape(count_dev, share, D),
        weight_block(mixed, d_first_b).reshape(count_dev, share, D),
        weight_block(hidden_b, d_pre_b).reshape(count_dev, inner_rows, D),
        weight_block(act_b, d_second_b).reshape(count_dev, outer_share, D),
    ]
    owned = lax.psum_scatter(
        (jnp.concatenate(pieces, 1) * factor).reshape(count_dev * per_dev, D),
        ("dp", "fsdp"),
        scatter_dimension=0,
        tiled=True,
    )
    small_owned = (
        lax.psum_scatter(small_terms[0], ("dp", "fsdp"), scatter_dimension=0, tiled=True),
        lax.psum_scatter(small_terms[1], ("dp", "fsdp"), scatter_dimension=0, tiled=True),
        lax.psum_scatter(small_terms[2], ("dp", "fsdp"), scatter_dimension=0, tiled=True),
        lax.psum_scatter(small_terms[3], ("dp", "fsdp"), scatter_dimension=0, tiled=True),
        lax.psum_scatter(small_terms[4], ("dp", "fsdp"), scatter_dimension=0, tiled=True),
        lax.psum_scatter(small_terms[5], ("dp", "fsdp"), scatter_dimension=0, tiled=True),
        lax.psum_scatter(small_terms[6], ("dp", "fsdp"), scatter_dimension=0, tiled=True),
        lax.psum_scatter(small_terms[7], ("dp", "fsdp"), scatter_dimension=0, tiled=True),
        lax.psum_scatter(small_terms[8], ("dp", "fsdp"), scatter_dimension=0, tiled=True),
    )
    grad_query_weight = owned[0:share]
    grad_key_weight = owned[share : 2 * share]
    grad_value_weight = owned[2 * share : 3 * share]
    grad_out_weight = owned[3 * share : 4 * share]
    grad_inner_weight = owned[4 * share : 4 * share + inner_rows].reshape(share, FF)
    grad_outer_weight = owned[4 * share + inner_rows : per_dev]
    return (
        layer_out,
        grad_tokens,
        grad_query_weight,
        small_owned[0],
        grad_key_weight,
        grad_value_weight,
        small_owned[1],
        grad_out_weight,
        small_owned[2],
        small_owned[3],
        small_owned[4],
        grad_inner_weight,
        small_owned[5],
        grad_outer_weight,
        small_owned[6],
        small_owned[7],
        small_owned[8],
    )


def solution(mesh):
    placed = (
        P(("dp", "fsdp"), None),
        P(("dp", "fsdp")),
        P(("dp", "fsdp"), None),
        P(("dp", "fsdp"), None),
        P(("dp", "fsdp")),
        P(("dp", "fsdp"), None),
        P(("dp", "fsdp"), None),
        P(("dp", "fsdp")),
        P(("dp", "fsdp"), None),
        P(("dp", "fsdp")),
        P(("dp", "fsdp")),
        P(("dp", "fsdp")),
        P(("dp", "fsdp"), None),
        P(("dp", "fsdp")),
        P(("dp", "fsdp"), None),
        P(("dp", "fsdp")),
        P(("dp", "fsdp")),
        P(("dp", "fsdp")),
    )
    return jax.shard_map(
        shards,
        mesh=mesh,
        in_specs=placed,
        out_specs=(
            P(("dp", "fsdp"), None),
            P(("dp", "fsdp"), None),
            P(("dp", "fsdp"), None),
            P(("dp", "fsdp")),
            P(("dp", "fsdp"), None),
            P(("dp", "fsdp"), None),
            P(("dp", "fsdp")),
            P(("dp", "fsdp"), None),
            P(("dp", "fsdp")),
            P(("dp", "fsdp")),
            P(("dp", "fsdp")),
            P(("dp", "fsdp"), None),
            P(("dp", "fsdp")),
            P(("dp", "fsdp"), None),
            P(("dp", "fsdp")),
            P(("dp", "fsdp")),
            P(("dp", "fsdp")),
        ),
        check_vma=False,
    )
```

profile of v0, /device:TPU:0, one launch (start us, length us, event | category | flops | bytes accessed | tf_op | source)
XLA Modules:
  0.0 730.6 jit_solution(14738238862979127013)
XLA Ops:
  7.2 0.7 all-gather.7.cloned.1.call-update
  8.0 0.7 all-gather.9.cloned.1.call-update
  8.7 0.7 all-gather.11.cloned.1.call-update
  11.2 0.8 dynamic-update-slice
  12.1 0.8 dynamic-update-slice.1
  12.9 0.8 dynamic-update-slice.2
  13.7 0.8 dynamic-update-slice.6
  14.6 0.8 dynamic-update-slice.4
  15.4 0.8 dynamic-update-slice.3
  16.3 0.8 dynamic-update-slice.8
  17.1 0.8 dynamic-update-slice.7
  17.9 0.8 dynamic-update-slice.5
  18.8 42.8 %all-reduce.19 = (bf16[768]{0:T(1024)(128)(2,1)S(1)}, bf16[768]{0:T(1024)(128)(2,1)S(1)}, bf16[768]{0:T(1024)(128)(2,1)S(1)}, bf16[768]{0:T(1024)(128)(2,1)S(1)}...) all-reduce(bf16[768]{0:T(1024)(128)(2,1)S(1)} %dynamic-update-slice, ...), channel_id=1, replica_groups=mesh['dp'=4,'fsdp'=8] {'dp','fsdp'}, use_global_device_ids=true, to_apply=%add | all-reduce | flops 9216 | bytes 36864
  61.5 0.6 convert_element_type.112
  62.8 0.6 convert_element_type.113
  63.4 0.6 convert_element_type.114
  64.0 4.0 all-gather.7.cloned.1.call-done
  68.1 1.7 fusion.12
  69.9 54.5 %all-gather.9.cloned.1.call-done = bf16[768,768]{1,0:T(8,128)(2,1)} async-done(((bf16[24,768]{1,0:T(8,128)(2,1)}), bf16[768,768]{1,0:T(8,128)(2,1)}) %all-gather.9.cloned.1.call-update) | async-done | bytes 1179664 | tf_op jit(solution)/shard_map/all_gather | solution.py:232
  124.5 1.6 fusion.13
  126.3 54.4 %all-gather.11.cloned.1.call-done = bf16[768,768]{1,0:T(8,128)(2,1)} async-done(((bf16[24,768]{1,0:T(8,128)(2,1)}), bf16[768,768]{1,0:T(8,128)(2,1)}) %all-gather.11.cloned.1.call-update) | async-done | bytes 1179664 | tf_op jit(solution)/shard_map/all_gather | solution.py:234
  180.7 1.6 convolution_convert_fusion.3
  183.2 53.5 %all-gather.13.cloned.1.call-done = bf16[768,768]{1,0:T(8,128)(2,1)} async-done(((bf16[24,768]{1,0:T(8,128)(2,1)}), bf16[768,768]{1,0:T(8,128)(2,1)}) %all-gather.13.cloned.1.call-update) | async-done | bytes 1179664 | tf_op jit(solution)/shard_map/all_gather | solution.py:237
  236.7 1.7 fusion.50
  238.6 63.5 %all-gather.15.cloned.1.call-done = bf16[768,3072]{1,0:T(8,128)(2,1)} async-done(((bf16[24,3072]{1,0:T(8,128)(2,1)}), bf16[768,3072]{1,0:T(8,128)(2,1)}) %all-gather.15.cloned.1.call-update) | async-done | bytes 4718608 | tf_op jit(solution)/shard_map/all_gather | solution.py:241
  302.2 3.2 convolution_add_fusion
  305.4 62.1 %all-gather.17.cloned.1.call-done = bf16[3072,768]{1,0:T(8,128)(2,1)} async-done(((bf16[96,768]{1,0:T(8,128)(2,1)}), bf16[3072,768]{1,0:T(8,128)(2,1)}) %all-gather.17.cloned.1.call-update) | async-done | bytes 4718608 | tf_op jit(solution)/shard_map/all_gather | solution.py:243
  367.6 3.5 fusion.51
  371.3 0.8 multiply_reduce_fusion.1
  372.1 1.5 fusion.43
  373.6 2.3 fusion.54
  376.0 2.3 multiply_reduce_fusion.2
  378.4 0.8 fusion.44
  379.6 1.2 convolution_convert_fusion.1
  380.9 1.7 copy.59
  382.6 2.2 fusion.55
  384.8 3.1 fusion.48
  387.9 2.6 convolution_convert_fusion
  390.5 2.1 fusion.47
  392.6 6.0 fusion.19
  398.5 5.1 fusion.34
  403.6 0.7 fusion.56
  404.4 1.5 constant_dynamic-update-slice_fusion.4
  406.0 2.0 fusion.57
  408.5 11.5 %reshape.158 = f32[32,96,768]{2,1,0:T(8,128)} reshape(f32[768,3072]{1,0:T(8,128)} %fusion.19) | data formatting | bytes 18874368 | tf_op jit(solution)/shard_map/reshape | solution.py:288
  420.0 3.4 constant_dynamic-update-slice_fusion.3
  423.4 1.7 constant_dynamic-update-slice_fusion.2
  425.1 1.9 convolution_dynamic-update-slice_fusion
  427.0 4.9 constant_dynamic-update-slice_fusion.1
  431.9 4.6 constant_dynamic-update-slice_fusion
  436.5 20.1 %broadcast_multiply_fusion = f32[32,288,768]{2,1,0:T(8,128)} fusion(f32[32,288,768]{2,1,0:T(8,128)} %constant_dynamic-update-slice_fusion), kind=kLoop, calls=%fused_computation.1 | loop fusion | flops 7077888 | bytes 56623104 | tf_op jit(solution)/shard_map/mul | solution.py:292
  457.6 40.5 %all-reduce.18 = (f32[768]{0:T(1024)S(1)}, f32[768]{0:T(1024)S(1)}, f32[768]{0:T(1024)S(1)}, f32[768]{0:T(1024)S(1)}, f32[768]{0:T(1024)S(1)}, /*index=5*/f32[30...) all-reduce(f32[768]{0:T(1024)S(1)} %mul.225, ...), channel_id=3, replica_groups=mesh['dp'=4,'fsdp'=8] {'dp','fsdp'}, use_global_device_ids=true, to_apply=%region_13.14.clone | all-reduce | flops 9216 | bytes 73728
  498.1 0.6 dynamic-slice
  498.7 0.6 dynamic-slice.1
  499.3 0.6 dynamic-slice.2
  499.8 0.6 dynamic-slice.3
  500.4 0.6 dynamic-slice.4
  502.7 0.6 dynamic-slice.5
  504.4 0.8 copy-done.5
  505.3 1.3 convolution_add_fusion.1
  506.6 212.9 %reduce-scatter.2.cloned.1.call-done = f32[288,768]{1,0:T(8,128)} async-done(((f32[9216,768]{1,0:T(8,128)}), f32[288,768]{1,0:T(8,128)}) %reduce-scatter.2.cloned.1.call-update) | async-done | bytes 884752 | tf_op jit(solution)/shard_map/reduce_scatter | solution.py:291
  719.4 1.8 fusion.45
  721.2 0.8 reshape.160
  722.0 1.7 fusion.46
  (146 shorter events, 8.2 us)
Async XLA Ops:
  7.2 117.3 %copy-start.1 = (bf16[128,768]{1,0:T(8,128)(2,1)S(1)}, bf16[128,768]{1,0:T(8,128)(2,1)}, u32[]{:S(2)}) copy-start(bf16[128,768]{1,0:T(8,128)(2,1)} %param.18) | copy-start | bytes 589828
  7.2 60.9 %all-gather.7.cloned.1.call-start = ((), (), s32[]{:S(2)}) async-start(), calls=%async_computation.1 | async-start | bytes 1216512 | tf_op jit(solution)/shard_map/all_gather | solution.py:235
  7.9 116.5 %all-gather.9.cloned.1.call-start = ((), (), s32[]{:S(2)}) async-start(), calls=%async_computation.2 | async-start | bytes 1216512 | tf_op jit(solution)/shard_map/all_gather | solution.py:232
  8.7 172.0 %all-gather.11.cloned.1.call-start = ((), (), s32[]{:S(2)}) async-start(), calls=%async_computation.3 | async-start | bytes 1216512 | tf_op jit(solution)/shard_map/all_gather | solution.py:234
  9.4 227.3 %all-gather.13.cloned.1.call-start = ((), (), s32[]{:S(2)}) async-start(), calls=%async_computation.4 | async-start | bytes 1216512 | tf_op jit(solution)/shard_map/all_gather | solution.py:237
  10.0 292.2 %all-gather.15.cloned.1.call-start = ((), (), s32[]{:S(2)}) async-start(), calls=%async_computation.5 | async-start | bytes 4866048 | tf_op jit(solution)/shard_map/all_gather | solution.py:241
  10.6 357.0 %all-gather.17.cloned.1.call-start = ((), (), s32[]{:S(2)}) async-start(), calls=%async_computation.6 | async-start | bytes 4866048 | tf_op jit(solution)/shard_map/all_gather | solution.py:243
  11.2 708.3 %reduce-scatter.2.cloned.1.call-start = ((), (), s32[]{:S(2)}) async-start(), calls=%async_computation.7 | async-start | bytes 29196288 | tf_op jit(solution)/shard_map/reduce_scatter | solution.py:291
  69.9 113.0 %copy-start.13 = (bf16[128,768]{0,1:T(8,128)(2,1)}, bf16[128,768]{0,1:T(8,128)(2,1)S(1)}, u32[]{:S(2)}) copy-start(bf16[128,768]{0,1:T(8,128)(2,1)S(1)} %copy.55) | copy-start | bytes 589828
  126.3 56.5 %copy-start.17 = (bf16[128,768]{0,1:T(8,128)(2,1)}, bf16[128,768]{0,1:T(8,128)(2,1)S(1)}, u32[]{:S(2)}) copy-start(bf16[128,768]{0,1:T(8,128)(2,1)S(1)} %copy.56) | copy-start | bytes 589828
  182.4 0.8 copy-start.18
  238.4 63.8 %copy-start.25 = (f32[128]{0:T(128)}, f32[128]{0:T(128)S(1)}, u32[]{:S(2)}) copy-start(f32[128]{0:T(128)S(1)} %broadcast_multiply_fusion.15) | copy-start | bytes 1540
  238.6 63.6 %copy-start.27 = (f32[128]{0:T(128)}, f32[128]{0:T(128)S(1)}, u32[]{:S(2)}) copy-start(f32[128]{0:T(128)S(1)} %add_rsqrt_fusion.1) | copy-start | bytes 1540
  305.4 65.9 %copy-start.16 = (f32[128,768]{1,0:T(8,128)S(1)}, f32[128,768]{1,0:T(8,128)}, u32[]{:S(2)}) copy-start(f32[128,768]{1,0:T(8,128)} %param.20) | copy-start | bytes 1179652
  367.6 3.7 copy-start.23
  367.6 4.5 copy-start.31
  367.6 6.0 copy-start.4
  372.1 3.9 slice-start.3
  373.6 2.4 copy-start.9
  373.6 2.4 slice-start.4
  373.6 2.4 copy-start.26
  373.6 2.4 copy-start.28
  376.0 2.4 copy-start.11
  378.4 1.3 copy-start.8
  379.1 45.9 %copy-start.2 = (f32[128,768]{1,0:T(8,128)}, f32[128,768]{1,0:T(8,128)S(1)}, u32[]{:S(2)}) copy-start(f32[128,768]{1,0:T(8,128)S(1)} %get-tuple-element.46) | copy-start | bytes 1179652
  390.5 2.1 copy-start.12
  392.6 15.4 %copy-start.14 = (bf16[128,12,64]{0,2,1:T(8,128)(2,1)}, bf16[128,12,64]{0,2,1:T(8,128)(2,1)S(1)}, u32[]{:S(2)}) copy-start(bf16[128,12,64]{0,2,1:T(8,128)(2,1)S(1)} %get-tuple-element.55) | copy-start | bytes 589828
  392.6 6.0 copy-start.10
  398.5 5.1 copy-start.21
  404.4 1.6 copy-start.19
  420.0 7.0 copy-start
  425.1 6.8 slice-start
  427.0 4.9 slice-start.1
  427.0 4.9 slice-start.2
  456.6 0.7 copy-start.37
  456.6 0.8 copy-start.24
  456.6 0.9 copy-start.30
  456.6 0.9 copy-start.35
  456.6 0.9 copy-start.34
  456.6 0.9 copy-start.29
  456.6 0.9 copy-start.32
  456.6 0.9 copy-start.33
  456.7 0.9 copy-start.36
  456.7 46.7 %copy-start.3 = (f32[128,768]{1,0:T(8,128)S(1)}, f32[128,768]{1,0:T(8,128)}, u32[]{:S(2)}) copy-start(f32[128,768]{1,0:T(8,128)} %copy-done.2) | copy-start | bytes 1179652
  456.7 46.7 %copy-start.6 = (bf16[768,768]{1,0:T(8,128)(2,1)S(1)}, bf16[768,768]{1,0:T(8,128)(2,1)}, u32[]{:S(2)}) copy-start(bf16[768,768]{1,0:T(8,128)(2,1)} %all-gather.9.cloned.1.call-done) | copy-start | bytes 3538948
  456.7 46.6 %copy-start.22 = (bf16[128,12,64]{0,2,1:T(8,128)(2,1)S(1)}, bf16[128,12,64]{0,2,1:T(8,128)(2,1)}, u32[]{:S(2)}) copy-start(bf16[128,12,64]{0,2,1:T(8,128)(2,1)} %get-tuple-element.57) | copy-start | bytes 589828
  456.7 47.1 %copy-start.7 = (bf16[768,768]{1,0:T(8,128)(2,1)S(1)}, bf16[768,768]{1,0:T(8,128)(2,1)}, u32[]{:S(2)}) copy-start(bf16[768,768]{1,0:T(8,128)(2,1)} %all-gather.11.cloned.1.call-done) | copy-start | bytes 3538948
  456.7 47.1 %copy-start.20 = (bf16[12,64,128]{2,1,0:T(8,128)(2,1)S(1)}, bf16[12,64,128]{2,1,0:T(8,128)(2,1)}, u32[]{:S(2)}) copy-start(bf16[12,64,128]{2,1,0:T(8,128)(2,1)} %convolution_convert_fusion) | copy-start | bytes 589828
  503.9 1.4 copy-start.5
  503.9 1.4 copy-start.15
Sparse Core Ops, SparseCore 0:
  11.1 56.9 all-gather.6
  71.1 53.3 all-gather.8
  127.5 53.1 all-gather.10
  183.5 53.1 all-gather.12
  239.6 62.5 all-gather.14
  305.1 62.4 all-gather.16
  456.8 262.5 reduce-scatter.1
where the time goes:
time: 732 us; the launch traced here: 731 us
  waiting for transfers between devices  509 us (70%)
  blocking collectives  83.3 us (11%)
  local copies, waits for them, and re-layouts  49.1 us (7%)
  matrix products  48.3 us (7%)
  other arithmetic  25.6 us (3%)
  between operations  15.4 us (2%)
    reduce_scatter x1, waiting for transfers between devices, shards(): lax.psum_scatter((jnp.concatenate(pieces, 1) * factor).reshape(count_dev...  213 us
    unnamed x2, blocking collectives  83.3 us
    all_gather x1, waiting for transfers between devices, shards(): lax.all_gather(inner_weight, ('dp', 'fsdp'), axis=0, tiled=True)  63.5 us
    all_gather x1, waiting for transfers between devices, shards(): lax.all_gather(outer_weight, ('dp', 'fsdp'), axis=0, tiled=True)  62.1 us
    all_gather x1, waiting for transfers between devices, shards(): lax.all_gather(query_weight, ('dp', 'fsdp'), axis=0, tiled=True)  54.5 us
    all_gather x1, waiting for transfers between devices, shards(): lax.all_gather(key_weight, ('dp', 'fsdp'), axis=0, tiled=True)  54.4 us
    all_gather x1, waiting for transfers between devices, shards(): lax.all_gather(out_weight, ('dp', 'fsdp'), axis=0, tiled=True)  53.5 us
    unnamed x117, local copies, waits for them, and re-layouts  26.4 us
  transfers between devices with their start and end apart: 7, of which 7 were waited for; matrix products, arithmetic and copies ran while one was open for 4% of the time, Pallas kernels for 0%

commit v1 on v0

--- a/solution.py
+++ b/solution.py
@@ -207,6 +207,26 @@
     return (grad_tokens, small, factors)
 
 
+def round_up(value, multiple):
+    return -(-value // multiple) * multiple
+
+
+def to_row(vectors, dtype):
+    flat = jnp.concatenate([v.astype(dtype) for v in vectors], -1)
+    lead = flat.shape[:-1]
+    pad = [(0, 0)] * len(lead) + [(0, D - flat.shape[-1])]
+    return jnp.pad(flat, pad).reshape(lead + (1, D))
+
+
+def gather_rows(block):
+    return lax.all_gather(block, ("dp", "fsdp"), axis=0)
+
+
+def scatter_rows(blocks):
+    owned = lax.psum_scatter(blocks, ("dp", "fsdp"), scatter_dimension=0, tiled=True)
+    return owned[0].astype(jnp.float32)
+
+
 def shards(
     tokens,
     lengths,
@@ -227,108 +247,119 @@
     norm2_gain,
     norm2_shift,
 ):
+    bf16 = jnp.bfloat16
     length = lengths[0]
+    share = query_weight.shape[0]
+    wide = FF // D
+    devices = lax.axis_size("dp") * lax.axis_size("fsdp")
+    used = (4 + 2 * wide) * share + 1
+    rows = round_up(used, 16)
+    packed = jnp.concatenate(
+        [query_weight, key_weight, value_weight, out_weight]
+        + [inner_weight[:, j * D : (j + 1) * D] for j in range(wide)]
+        + [
+            outer_weight,
+            to_row(
+                [
+                    query_bias,
+                    value_bias,
+                    out_bias,
+                    norm1_gain,
+                    norm1_shift,
+                    outer_bias,
+                    norm2_gain,
+                    norm2_shift,
+                    inner_bias,
+                ],
+                bf16,
+            ),
+            jnp.zeros((rows - used, D), bf16),
+        ],
+        0,
+    )
+    every = gather_rows(packed)
+
+    def matrix(start, count):
+        return every[:, start * share : (start + count) * share].reshape(-1, D)
+
+    small = every[:, used - 1]
+
+    def vector(start, count=1):
+        return small[:, start * share : (start + count) * share].reshape(-1)
+
     whole = (
-        lax.all_gather(query_weight, ("dp", "fsdp"), axis=0, tiled=True),
-        lax.all_gather(query_bias, ("dp", "fsdp"), axis=0, tiled=True),
-        lax.all_gather(key_weight, ("dp", "fsdp"), axis=0, tiled=True),
-        lax.all_gather(value_weight, ("dp", "fsdp"), axis=0, tiled=True),
-        lax.all_gather(value_bias, ("dp", "fsdp"), axis=0, tiled=True),
-        lax.all_gather(out_weight, ("dp", "fsdp"), axis=0, tiled=True),
-        lax.all_gather(out_bias, ("dp", "fsdp"), axis=0, tiled=True),
-        lax.all_gather(norm1_gain, ("dp", "fsdp"), axis=0, tiled=True),
-        lax.all_gather(norm1_shift, ("dp", "fsdp"), axis=0, tiled=True),
-        lax.all_gather(inner_weight, ("dp", "fsdp"), axis=0, tiled=True),
-        lax.all_gather(inner_bias, ("dp", "fsdp"), axis=0, tiled=True),
-        lax.all_gather(outer_weight, ("dp", "fsdp"), axis=0, tiled=True),
-        lax.all_gather(outer_bias, ("dp", "fsdp"), axis=0, tiled=True),
-        lax.all_gather(norm2_gain, ("dp", "fsdp"), axis=0, tiled=True),
-        lax.all_gather(norm2_shift, ("dp", "fsdp"), axis=0, tiled=True),
+        matrix(0, 1),
+        vector(0),
+        matrix(1, 1),
+        matrix(2, 1),
+        vector(1),
+        matrix(3, 1),
+        vector(2),
+        vector(3),
+        vector(4),
+        jnp.concatenate([matrix(4 + j, 1) for j in range(wide)], 1),
+        vector(8, wide),
+        matrix(4 + wide, wide),
+        vector(5),
+        vector(6),
+        vector(7),
     )
     layer_out, saved = forward_pass(tokens, length, whole)
-    weights_back = (
-        lax.all_gather(query_weight, ("dp", "fsdp"), axis=0, tiled=True),
-        lax.all_gather(query_bias, ("dp", "fsdp"), axis=0, tiled=True),
-        lax.all_gather(key_weight, ("dp", "fsdp"), axis=0, tiled=True),
-        lax.all_gather(value_weight, ("dp", "fsdp"), axis=0, tiled=True),
-        lax.all_gather(value_bias, ("dp", "fsdp"), axis=0, tiled=True),
-        lax.all_gather(out_weight, ("dp", "fsdp"), axis=0, tiled=True),
-        lax.all_gather(out_bias, ("dp", "fsdp"), axis=0, tiled=True),
-        lax.all_gather(norm1_gain, ("dp", "fsdp"), axis=0, tiled=True),
-        lax.all_gather(norm1_shift, ("dp", "fsdp"), axis=0, tiled=True),
-        lax.all_gather(inner_weight, ("dp", "fsdp"), axis=0, tiled=True),
-        lax.all_gather(inner_bias, ("dp", "fsdp"), axis=0, tiled=True),
-        lax.all_gather(outer_weight, ("dp", "fsdp"), axis=0, tiled=True),
-        lax.all_gather(outer_bias, ("dp", "fsdp"), axis=0, tiled=True),
-        lax.all_gather(norm2_gain, ("dp", "fsdp"), axis=0, tiled=True),
-        lax.all_gather(norm2_shift, ("dp", "fsdp"), axis=0, tiled=True),
-    )
-    grad_tokens, small, factors = backward_pass(tokens, cotangent, length, weights_back, saved)
+    grad_tokens, sums, factors = backward_pass(tokens, cotangent, length, whole, saved)
     tok_rows, d_query, d_keys, d_values, mixed, d_first_b, hidden_b, d_pre_b, act_b, d_second_b = (
         factors
     )
-    devices = lax.axis_size("dp") * lax.axis_size("fsdp")
-    total_rows = tokens.shape[0] * devices
-    factor = 1.0 / jnp.sqrt(jnp.float32(total_rows))
-    share = D // devices
-    outer_share = FF // devices
-    inner_rows = share * FF // D
-    per_dev = 4 * share + inner_rows + outer_share
+    factor = 1.0 / jnp.sqrt(jnp.float32(tokens.shape[0] * devices))
 
     def weight_block(left, right):
-        return jnp.dot(left.T, right, preferred_element_type=jnp.float32)
-
-    small_terms = tuple((g * factor for g in small))
-    count_dev = per_dev * lax.axis_size(("dp", "fsdp")) // per_dev
-    pieces = [
-        weight_block(tok_rows, d_query).reshape(count_dev, share, D),
-        weight_block(tok_rows, d_keys).reshape(count_dev, share, D),
-        weight_block(tok_rows, d_values).reshape(count_dev, share, D),
-        weight_block(mixed, d_first_b).reshape(count_dev, share, D),
-        weight_block(hidden_b, d_pre_b).reshape(count_dev, inner_rows, D),
-        weight_block(act_b, d_second_b).reshape(count_dev, outer_share, D),
-    ]
-    owned = lax.psum_scatter(
-        (jnp.concatenate(pieces, 1) * factor).reshape(count_dev * per_dev, D),
-        ("dp", "fsdp"),
-        scatter_dimension=0,
-        tiled=True,
-    )
-    small_owned = (
-        lax.psum_scatter(small_terms[0], ("dp", "fsdp"), scatter_dimension=0, tiled=True),
-        lax.psum_scatter(small_terms[1], ("dp", "fsdp"), scatter_dimension=0, tiled=True),
-        lax.psum_scatter(small_terms[2], ("dp", "fsdp"), scatter_dimension=0, tiled=True),
-        lax.psum_scatter(small_terms[3], ("dp", "fsdp"), scatter_dimension=0, tiled=True),
-        lax.psum_scatter(small_terms[4], ("dp", "fsdp"), scatter_dimension=0, tiled=True),
-        lax.psum_scatter(small_terms[5], ("dp", "fsdp"), scatter_dimension=0, tiled=True),
-        lax.psum_scatter(small_terms[6], ("dp", "fsdp"), scatter_dimension=0, tiled=True),
-        lax.psum_scatter(small_terms[7], ("dp", "fsdp"), scatter_dimension=0, tiled=True),
-        lax.psum_scatter(small_terms[8], ("dp", "fsdp"), scatter_dimension=0, tiled=True),
-    )
-    grad_query_weight = owned[0:share]
-    grad_key_weight = owned[share : 2 * share]
-    grad_value_weight = owned[2 * share : 3 * share]
-    grad_out_weight = owned[3 * share : 4 * share]
-    grad_inner_weight = owned[4 * share : 4 * share + inner_rows].reshape(share, FF)
-    grad_outer_weight = owned[4 * share + inner_rows : per_dev]
+        block = lax.dot_general(
+            left, right, (((0,), (0,)), ((), ())), preferred_element_type=jnp.float32
+        )
+        return block.astype(bf16).reshape(devices, -1, D)
+
+    split = [g.reshape(devices, -1) for g in sums]
+    order = (0, 1, 2, 3, 4, 6, 7, 8, 5)
+    terms = jnp.concatenate(
+        [
+            weight_block(tok_rows, d_query),
+            weight_block(tok_rows, d_keys),
+            weight_block(tok_rows, d_values),
+            weight_block(mixed, d_first_b),
+        ]
+        + [weight_block(hidden_b, d_pre_b[:, j * D : (j + 1) * D]) for j in range(wide)]
+        + [
+            weight_block(act_b, d_second_b),
+            to_row([split[i] for i in order], bf16),
+            jnp.zeros((devices, rows - used, D), bf16),
+        ],
+        1,
+    )
+    owned = scatter_rows(terms) * factor
+
+    def mine(start, count=1):
+        return owned[start * share : (start + count) * share]
+
+    def mine_small(start, count=1):
+        return owned[used - 1, start * share : (start + count) * share]
+
     return (
         layer_out,
         grad_tokens,
-        grad_query_weight,
-        small_owned[0],
-        grad_key_weight,
-        grad_value_weight,
-        small_owned[1],
-        grad_out_weight,
-        small_owned[2],
-        small_owned[3],
-        small_owned[4],
-        grad_inner_weight,
-        small_owned[5],
-        grad_outer_weight,
-        small_owned[6],
-        small_owned[7],
-        small_owned[8],
+        mine(0),
+        mine_small(0),
+        mine(1),
+        mine(2),
+        mine_small(1),
+        mine(3),
+        mine_small(2),
+        mine_small(3),
+        mine_small(4),
+        jnp.concatenate([mine(4 + j) for j in range(wide)], 1),
+        mine_small(8, wide),
+        mine(4 + wide, wide),
+        mine_small(5),
+        mine_small(6),
+        mine_small(7),
     )
 
 

time: 732 us -> 467 us (0.64)
  waiting for transfers between devices: 509 us -> 269 us
  blocking collectives: 83.3 us -> 0 us
  local copies, waits for them, and re-layouts: 49.1 us -> 132 us
  other arithmetic: 25.6 us -> 7.5 us
  matrix products: 48.3 us -> 40.6 us
    all_gather x6 -> x1, waiting for transfers between devices: 292 us -> 108 us  [gather_rows(): return lax.all_gather(block, ('dp', 'fsdp'), axis=0)]
    concatenate x1 -> x4, local copies, waits for them, and re-layouts: 4.58 us -> 93.6 us  [the longest x1 76 us: shards(): jnp.concatenate([weight_block(tok_rows, d_query), weight_block(tok_rows,...]
    unnamed x2 -> x0, blocking collectives: 83.3 us -> none
    reduce_scatter x1, waiting for transfers between devices: 213 us -> 160 us  [scatter_rows(): lax.psum_scatter(blocks, ('dp', 'fsdp'), scatter_dimension=0, tiled=True)]
    unnamed x117 -> x83, local copies, waits for them, and re-layouts: 26.4 us -> 5.34 us
    mul x9 -> x1, other arithmetic: 20.2 us -> 1.14 us  [shards(): owned = scatter_rows(terms) * factor]
    convert_element_type x3 -> x18, local copies, waits for them, and re-layouts: 0.48 us -> 14.2 us  [the longest x9 4.14 us: to_row(): flat = jnp.concatenate([v.astype(dtype) for v in vectors], -1)]
    reshape x2 -> x3, local copies, waits for them, and re-layouts: 12.3 us -> 0.73 us  [to_row(): return jnp.pad(flat, pad).reshape(lead + (1, D))]
  transfers between devices with their start and end apart: 7 -> 2, of which waited for: 7 -> 2; matrix products, arithmetic and copies ran while one was open for 4% -> 1% of each run, Pallas kernels for 0% -> 0%
where the time goes in v1:
time: 467 us; the launch traced here: 464 us
  waiting for transfers between devices  269 us (58%)
  local copies, waits for them, and re-layouts  132 us (28%)
  matrix products  40.6 us (9%)
  between operations  15.2 us (3%)
  other arithmetic  7.5 us (2%)
    reduce_scatter x1, waiting for transfers between devices, scatter_rows(): lax.psum_scatter(blocks, ('dp', 'fsdp'), scatter_dimension=0, tiled=True)  160 us
    all_gather x1, waiting for transfers between devices, gather_rows(): return lax.all_gather(block, ('dp', 'fsdp'), axis=0)  108 us
    concatenate x1, local copies, waits for them, and re-layouts, shards(): jnp.concatenate([weight_block(tok_rows, d_query), weight_block(tok_rows,...  76 us
    dot_general x9, matrix products, weight_block(): lax.dot_general(left, right, (((0,), (0,)), ((), ())), preferred_element_...  17.3 us
    concatenate x1, local copies, waits for them, and re-layouts, shards(): jnp.concatenate([query_weight, key_weight, value_weight, out_weight] + [i...  11.5 us
    slice x2, local copies, waits for them, and re-layouts, matrix(): return every[:, start * share:(start + count) * share].reshape(-1, D)  11.3 us
  transfers between devices with their start and end apart: 2, of which 2 were waited for; matrix products, arithmetic and copies ran while one was open for 1% of the time, Pallas kernels for 0%

profile of v1, /device:TPU:0, one launch (start us, length us, event | category | flops | bytes accessed | tf_op | source)
XLA Modules:
  0.0 463.6 jit_solution(7615268829440400065)
XLA Ops:
  7.2 6.1 %concatenate.18 = bf16[288]{0:T(512)(128)(2,1)S(1)} concatenate(bf16[24]{0:T(256)(128)(2,1)} %param.22, bf16[24]{0:T(256)(128)(2,1)} %param.25, bf16[24]{0:T(256)(128)(2,1)} %param.27, bf16[24]{0:T(256)(128)(2,1)} %param.28, bf16[24]{0:T(256)(128)(2,1)} %param.29, bf16[24]{0:T(256)(128)(2,1)} %param.33, bf16[24]{0:T(256)(128)(2,1)} %param.34, bf16[24]{0:T(256)(128)(2,1)} %param.35, ...), dimensions={0} | concatenate | bytes 1152 | tf_op jit(solution)/shard_map/concatenate | solution.py:215
  13.4 0.8 fusion.49
  14.2 11.5 %concatenate.19 = bf16[304,768]{1,0:T(8,128)(2,1)} concatenate(bf16[24,768]{1,0:T(8,128)(2,1)} %param.21, bf16[24,768]{1,0:T(8,128)(2,1)} %param.23, bf16[24,768]{1,0:T(8,128)(2,1)} %param.24, bf16[24,768]{1,0:T(8,128)(2,1)} %param.26, bf16[24,768]{1,0:T(8,128)(2,1)S(1)} %get-tuple-element.64, bf16[24,768]{1,0:T(8,128)(2,1)S(1)} %get-tuple-element.63, ...), dimensions={0} | concatenate | bytes 933888 | tf_op jit(solution)/shard_map/concatenate | solution.py:257
  26.4 0.5 iota_compare_fusion
  26.9 108.3 %all-gather.3.cloned.1.call-done = bf16[9728,768]{1,0:T(8,128)(2,1)} async-done(((bf16[304,768]{1,0:T(8,128)(2,1)}), bf16[9728,768]{1,0:T(8,128)(2,1)}) %all-gather.3.cloned.1.call-update) | async-done | bytes 14942224 | tf_op jit(solution)/shard_map/all_gather | solution.py:222
  135.2 1.0 slice.217
  136.2 0.7 slice_convert_fusion.3
  136.9 0.7 slice_convert_fusion.1
  137.6 4.8 %slice.231 = bf16[32,96,768]{2,1,0:T(8,128)(2,1)} slice(bf16[32,304,768]{2,1,0:T(8,128)(2,1)} %bitcast.136), slice={[0:32], [192:288], [0:768]} | slice | bytes 9437184 | tf_op jit(solution)/shard_map/slice | solution.py:283
  142.4 6.5 %fusion.45 = (bf16[32,24,768]{2,1,0:T(8,128)(2,1)}, bf16[32,24,768]{2,1,0:T(8,128)(2,1)}, bf16[32,24,768]{2,1,0:T(8,128)(2,1)}, bf16[32,24,768]{2,1,0:T(8,128)(2...) fusion(bf16[32,304,768]{2,1,0:T(8,128)(2,1)} %bitcast.137), kind=kLoop, calls=%fused_computation.127 | loop fusion | bytes 18874368 | tf_op jit(solution)/shard_map/slice | solution.py:283
  148.9 1.4 reshape.311
  150.4 0.7 reshape.313
  151.0 0.8 reshape.309
  151.8 0.8 reshape.310
  152.6 1.4 reshape.314
  154.0 1.4 reshape.312
  155.4 1.4 reshape.308
  156.8 0.8 reshape.307
  157.6 1.4 reshape.306
  159.0 1.5 convolution_convert_fusion.12
  160.6 0.5 fusion.13
  164.5 0.8 convolution_add_fusion
  165.4 0.8 slice-done
  166.2 1.0 fusion.52
  167.4 0.8 multiply_reduce_fusion.1
  168.2 1.5 fusion.43
  169.7 2.3 fusion.46
  172.0 2.3 multiply_reduce_fusion.2
  174.4 0.8 fusion.44
  175.1 0.7 copy-done.7
  175.9 1.2 convolution_convert_fusion.10
  177.1 1.7 copy.48
  178.8 2.0 fusion.47
  180.8 2.2 fusion.55
  183.1 2.5 convolution_convert_fusion.9
  185.5 3.1 fusion.48
  188.6 2.6 convolution_convert_fusion.5
  191.3 1.6 convolution_convert_fusion.1
  192.9 1.6 convolution_convert_fusion.2
  194.5 1.5 convolution_convert_fusion.3
  196.0 1.5 convolution_convert_fusion.4
  197.5 3.8 convolution_convert_fusion
  201.5 0.8 convert_element_type.344
  202.3 0.8 convert_element_type.332
  203.2 0.8 convert_element_type.334
  203.9 0.7 convert_element_type.336
  204.7 0.8 convert_element_type.328
  205.6 0.7 copy.52
  206.4 1.5 convolution_convert_fusion.6
  207.9 1.6 convolution_convert_fusion.7
  209.5 1.5 convolution_convert_fusion.8
  211.1 76.0 %concatenate.22 = bf16[32,304,768]{2,1,0:T(8,128)(2,1)} concatenate(bf16[32,24,768]{2,1,0:T(8,128)(2,1)} %bitcast.153, bf16[32,24,768]{2,1,0:T(8,128)(2,1)} %bitcast.152, bf16[32,24,768]{2,1,0:T(8,128)(2,1)} %bitcast.151, bf16[32,24,768]{2,1,0:T(8,128)(2,1)S(1)} %bitcast.146, bf16[32,24,768]{2,1,0:T(8,128)(2,1)} %bitcast.150, bf16[32,24,768]{2,1,0:T(8,128)(2,1)} %bitcast.149, ...), dimensions={1} | concatenate | bytes 29884416 | tf_op jit(solution)/shard_map/concatenate | solution.py:322
  287.1 1.2 copy-done.3
  288.5 0.5 convolution_add_fusion.3
  289.0 0.7 copy-done.1
  289.7 0.5 convolution_add_fusion.2
  290.7 1.3 convolution_add_fusion.1
  291.9 160.2 %reduce-scatter.2.cloned.1.call-done = bf16[1,304,768]{2,1,0:T(8,128)(2,1)} async-done(((bf16[32,304,768]{2,1,0:T(8,128)(2,1)}), bf16[1,304,768]{2,1,0:T(8,128)(2,1)}) %reduce-scatter.2.cloned.1.call-update) | async-done | bytes 466960 | tf_op jit(solution)/shard_map/reduce_scatter | solution.py:226
  452.2 1.1 fusion.30
  453.3 0.6 slice_bitcast_fusion.12
  453.9 0.6 slice_bitcast_fusion.9
  454.5 0.7 slice_bitcast_fusion
  455.3 0.7 slice_bitcast_fusion.4
  456.0 0.7 pad_maximum_fusion.3
  (110 shorter events, 4.7 us)
Async XLA Ops:
  7.2 128.0 %all-gather.3.cloned.1.call-start = ((), (), s32[]{:S(2)}) async-start(), calls=%async_computation.2 | async-start | bytes 15409152 | tf_op jit(solution)/shard_map/all_gather | solution.py:222
  25.7 426.5 %reduce-scatter.2.cloned.1.call-start = ((), (), s32[]{:S(2)}) async-start(), calls=%async_computation.1 | async-start | bytes 15409152 | tf_op jit(solution)/shard_map/reduce_scatter | solution.py:226
  148.9 12.2 %copy-start = (bf16[32,24,768]{2,1,0:T(8,128)(2,1)}, bf16[32,24,768]{2,1,0:T(8,128)(2,1)S(1)}, u32[]{:S(2)}) copy-start(bf16[32,24,768]{2,1,0:T(8,128)(2,1)S(1)} %get-tuple-element.34) | copy-start | bytes 3538948
  148.9 12.2 %copy-start.2 = (bf16[32,24,768]{2,1,0:T(8,128)(2,1)}, bf16[32,24,768]{2,1,0:T(8,128)(2,1)S(1)}, u32[]{:S(2)}) copy-start(bf16[32,24,768]{2,1,0:T(8,128)(2,1)S(1)} %get-tuple-element.35) | copy-start | bytes 3538948
  159.0 1.5 copy-start.5
  159.0 2.1 copy-start.38
  160.6 1.1 copy-start.28
  160.6 1.2 copy-start.34
  161.1 0.7 copy-start.29
  161.5 2.4 copy-start.22
  161.6 1.4 copy-start.4
  161.6 1.3 copy-start.33
  162.3 1.1 copy-start.15
  162.3 1.5 copy-start.21
  162.6 1.2 copy-start.14
  162.6 1.6 copy-start.19
  162.6 1.9 copy-start.20
  162.6 1.9 copy-start.35
  163.7 2.5 slice-start
  163.8 1.5 copy-start.9
  164.5 1.6 slice-start.1
  164.5 1.6 copy-start.32
  166.1 1.2 copy-start.18
  166.2 1.3 copy-start.30
  166.2 2.0 copy-start.31
  169.7 2.3 copy-start.16
  172.0 2.3 copy-start.23
  175.1 0.7 copy-start.7
  188.6 2.6 copy-start.10
  188.6 2.6 copy-start.24
  194.5 3.1 copy-start.17
  197.5 3.8 copy-start.37
  197.5 5.5 %copy-start.36 = (bf16[768]{0:T(1024)(128)(2,1)S(1)}, bf16[768]{0:T(1024)(128)(2,1)}, u32[]{:S(2)}) copy-start(bf16[768]{0:T(1024)(128)(2,1)} %get-tuple-element.25) | copy-start | bytes 4612
  197.5 8.8 %copy-start.6 = (bf16[128,768]{1,0:T(8,128)(2,1)S(1)}, bf16[128,768]{1,0:T(8,128)(2,1)}, u32[]{:S(2)}) copy-start(bf16[128,768]{1,0:T(8,128)(2,1)} %param.18) | copy-start | bytes 589828
  197.5 8.8 %copy-start.12 = (bf16[128,12,64]{0,2,1:T(8,128)(2,1)S(1)}, bf16[128,12,64]{0,2,1:T(8,128)(2,1)}, u32[]{:S(2)}) copy-start(bf16[128,12,64]{0,2,1:T(8,128)(2,1)} %get-tuple-element.59) | copy-start | bytes 589828
  201.3 6.6 %copy-start.25 = (bf16[12,64,128]{2,1,0:T(8,128)(2,1)S(1)}, bf16[12,64,128]{2,1,0:T(8,128)(2,1)}, u32[]{:S(2)}) copy-start(bf16[12,64,128]{2,1,0:T(8,128)(2,1)} %convolution_convert_fusion.9) | copy-start | bytes 589828
  206.4 3.1 copy-start.26
  209.5 1.6 copy-start.11
  287.1 1.3 copy-start.3
  287.1 1.3 copy-start.8
  287.1 1.4 copy-start.27
  288.5 1.3 copy-start.1
  289.7 0.9 copy-start.13
Sparse Core Ops, SparseCore 0:
  25.8 109.3 all-gather.2
  287.2 164.8 reduce-scatter.1

commit v2 on v1

--- a/solution.py
+++ b/solution.py
@@ -1,6 +1,11 @@
+import functools
+import math
+
 import jax
 import jax.numpy as jnp
 from jax import lax
+from jax.experimental import pallas as pl
+from jax.experimental.pallas import tpu as pltpu
 from jax.sharding import PartitionSpec as P
 
 D = 768
@@ -207,24 +212,281 @@
     return (grad_tokens, small, factors)
 
 
-def round_up(value, multiple):
-    return -(-value // multiple) * multiple
-
-
-def to_row(vectors, dtype):
-    flat = jnp.concatenate([v.astype(dtype) for v in vectors], -1)
-    lead = flat.shape[:-1]
-    pad = [(0, 0)] * len(lead) + [(0, D - flat.shape[-1])]
-    return jnp.pad(flat, pad).reshape(lead + (1, D))
-
-
-def gather_rows(block):
-    return lax.all_gather(block, ("dp", "fsdp"), axis=0)
-
-
-def scatter_rows(blocks):
-    owned = lax.psum_scatter(blocks, ("dp", "fsdp"), scatter_dimension=0, tiled=True)
-    return owned[0].astype(jnp.float32)
+MESH = pl.DeviceIdType.MESH
+LANES = 128
+
+
+class Place:
+    def __init__(self, side, depth):
+        self.side, self.depth = side, depth
+        dp, fsdp = lax.axis_index("dp"), lax.axis_index("fsdp")
+        self.c = fsdp % 2
+        self.z = fsdp // 2
+        row, col = dp // side, dp % side
+        self.a = (1 - self.c) * col + self.c * row
+        self.b = (1 - self.c) * row + self.c * col
+        self.dp = dp
+
+    def column(self, a, b, c):
+        return (1 - c) * (b * self.side + a) + c * (a * self.side + b)
+
+    def device(self, da=0, db=0, dz=0):
+        a, b = (self.a + da) % self.side, (self.b + db) % self.side
+        z = (self.z + dz) % self.depth
+        return (self.column(a, b, self.c), z * 2 + self.c)
+
+    def block(self, da, db, dz):
+        dp, fsdp = self.device(da, db, dz)
+        return dp * (2 * self.depth) + fsdp
+
+    def sibling(self):
+        return (self.dp, self.z * 2 + 1 - self.c)
+
+    def sibling_block(self, da, db, dz):
+        c = 1 - self.c
+        a, b = (self.b + da) % self.side, (self.a + db) % self.side
+        z = (self.z + dz) % self.depth
+        return self.column(a, b, c) * (2 * self.depth) + z * 2 + c
+
+
+def meet(place):
+    barrier = pltpu.get_barrier_semaphore()
+    others = [place.device(da=k) for k in range(1, place.side)]
+    others += [place.device(db=k) for k in range(1, place.side)]
+    others += [place.device(dz=k) for k in range(1, place.depth)]
+    others.append(place.sibling())
+    for other in others:
+        pl.semaphore_signal(barrier, inc=1, device_id=other, device_id_type=MESH)
+    pl.semaphore_wait(barrier, len(others))
+
+
+def gather_kernel(side, depth, a_ref, b_ref, a_out, b_out, keep, sent, got):
+    place = Place(side, depth)
+    meet(place)
+    pairs = ((a_ref, a_out), (b_ref, b_out))
+    me = place.block(0, 0, 0)
+    own = [
+        pltpu.make_async_copy(src.at[0], dst.at[me], keep.at[i])
+        for i, (src, dst) in enumerate(pairs)
+    ]
+    for copy in own:
+        copy.start()
+    started = []
+    half = side * side * depth
+
+    def slot(da, db, dz):
+        return (db * side + da) * depth + dz
+
+    def push(source, device, at, index, sem_at):
+        for i, (src, dst) in enumerate(pairs):
+            origin = src.at[0] if source is None else dst.at[source]
+            copy = pltpu.make_async_remote_copy(
+                src_ref=origin,
+                dst_ref=dst.at[at],
+                send_sem=sent.at[i, len(started) // 2],
+                recv_sem=got.at[i, sem_at],
+                device_id=device,
+                device_id_type=MESH,
+            )
+            copy.start()
+            started.append(copy)
+
+    def landed(index, sem_at):
+        for i, (src, dst) in enumerate(pairs):
+            pltpu.make_async_copy(dst.at[index], dst.at[index], got.at[i, sem_at]).wait()
+
+    def spread(source, da, db, dz):
+        index = place.block(da, db, dz)
+        if da == 0 and db == 0:
+            for k in range(1, side):
+                push(source, place.device(da=k), index, index, slot((side - k) % side, 0, dz))
+        if db == 0:
+            for k in range(1, side):
+                push(source, place.device(db=k), index, index, slot(da, (side - k) % side, dz))
+        push(source, place.sibling(), index, index, half + slot(da, db, dz))
+
+    for dz in range(1, depth):
+        push(None, place.device(dz=dz), me, me, slot(0, 0, depth - dz))
+    spread(None, 0, 0, 0)
+    near = sorted(range(1, depth), key=lambda k: min(k, depth - k))
+    steps = []
+    for rank, dz in enumerate([0] + near):
+        for db in range(side):
+            for da in range(side):
+                if (da, db, dz) != (0, 0, 0):
+                    steps.append((rank + (da > 0) + 2 * (db > 0), da, db, dz))
+    for _, da, db, dz in sorted(steps):
+        index = place.block(da, db, dz)
+        landed(index, slot(da, db, dz))
+        spread(index, da, db, dz)
+    for db in range(side):
+        for da in range(side):
+            for dz in range(depth):
+                landed(place.sibling_block(da, db, dz), half + slot(da, db, dz))
+    for copy in own:
+        copy.wait()
+    for copy in started:
+        copy.wait_send()
+
+
+def kernels_fit():
+    side = math.isqrt(lax.axis_size("dp"))
+    devices = lax.axis_size("dp") * lax.axis_size("fsdp")
+    return side * side == lax.axis_size("dp") and lax.axis_size("fsdp") % 2 == 0 and devices <= 32
+
+
+def gather_blocks(a_block, b_block):
+    if not kernels_fit():
+        return tuple(lax.all_gather(v, ("dp", "fsdp"), axis=0) for v in (a_block, b_block))
+    side, depth = math.isqrt(lax.axis_size("dp")), lax.axis_size("fsdp") // 2
+    devices = 2 * side * side * depth
+    anywhere = pl.BlockSpec(memory_space=pl.ANY)
+    return pl.pallas_call(
+        functools.partial(gather_kernel, side, depth),
+        name="gather_blocks",
+        out_shape=tuple(
+            jax.ShapeDtypeStruct((devices,) + v.shape, v.dtype) for v in (a_block, b_block)
+        ),
+        in_specs=[anywhere] * 2,
+        out_specs=(anywhere,) * 2,
+        scratch_shapes=[
+            pltpu.SemaphoreType.DMA((2,)),
+            pltpu.SemaphoreType.DMA((2, devices)),
+            pltpu.SemaphoreType.DMA((2, devices)),
+        ],
+        compiler_params=pltpu.CompilerParams(collective_id=0, has_side_effects=True),
+    )(a_block[None], b_block[None])
+
+
+def scatter_kernel(side, depth, a_in, b_in, a_out, b_out, *scratch):
+    a_bufs, b_bufs = scratch[0:4], scratch[4:8]
+    sent, got = scratch[8:10]
+    place = Place(side, depth)
+    meet(place)
+    started = []
+    half = side * side * depth
+    first2 = half
+    first3 = first2 + (side - 1) * side * depth
+    first4 = first3 + (side - 1) * depth
+    groups = ((a_in, a_bufs, a_out), (b_in, b_bufs, b_out))
+
+    def slot(da, db, dz):
+        return (db * side + da) * depth + dz
+
+    def push(pick_source, level, at, device, sem_at):
+        for i, (data, bufs, _) in enumerate(groups):
+            copy = pltpu.make_async_remote_copy(
+                src_ref=pick_source(data, bufs),
+                dst_ref=bufs[level].at[at],
+                send_sem=sent.at[i, len(started) // 2],
+                recv_sem=got.at[i, sem_at],
+                device_id=device,
+                device_id_type=MESH,
+            )
+            copy.start()
+            started.append(copy)
+
+    def landed(level, at, sem_at):
+        for i, (_, bufs, _) in enumerate(groups):
+            ref = bufs[level].at[at]
+            pltpu.make_async_copy(ref, ref, got.at[i, sem_at]).wait()
+
+    def add(k, block, extra, final=False):
+        for data, bufs, out in groups:
+            rows, lanes = data.shape[1:]
+            wide = lanes > D
+            step = lanes // 7 if wide else rows // 6
+            count = 7 if wide else 6
+
+            def body(n, _):
+                if wide:
+                    at = (slice(None), pl.ds(pl.multiple_of(n * step, LANES), step))
+                else:
+                    at = (pl.ds(pl.multiple_of(n * step, 16), step), slice(None))
+                total = bufs[0][(k,) + at].astype(jnp.float32)
+                total += data[(block,) + at].astype(jnp.float32)
+                for level, e in extra:
+                    total += bufs[level][(e,) + at].astype(jnp.float32)
+                if final:
+                    out[at] = total
+                else:
+                    bufs[0][(k,) + at] = total.astype(jnp.bfloat16)
+                return 0
+
+            lax.fori_loop(0, count, body, 0)
+
+    order = [
+        (da, db, dz)
+        for db in range(side - 1, -1, -1)
+        for da in range(side - 1, -1, -1)
+        for dz in range(depth - 1, -1, -1)
+    ]
+    for da, db, dz in order:
+        index = place.sibling_block(da, db, dz)
+        k = slot(da, db, dz)
+        push(lambda data, bufs: data.at[index], 0, k, place.sibling(), k)
+    for da, db, dz in order:
+        k = slot(da, db, dz)
+        landed(0, k, k)
+        extra = []
+        if db == 0:
+            for d in range(1, side):
+                e = (d - 1) * side * depth + da * depth + dz
+                landed(1, e, first2 + e)
+                extra.append((1, e))
+        if db == 0 and da == 0:
+            for d in range(1, side):
+                e = (d - 1) * depth + dz
+                landed(2, e, first3 + e)
+                extra.append((2, e))
+        if (da, db, dz) == (0, 0, 0):
+            for d in range(1, depth):
+                landed(3, d - 1, first4 + d - 1)
+                extra.append((3, d - 1))
+        add(k, place.block(da, db, dz), extra, final=(da, db, dz) == (0, 0, 0))
+        source = lambda data, bufs: bufs[0].at[k]
+        if db:
+            e = (db - 1) * side * depth + da * depth + dz
+            push(source, 1, e, place.device(db=db), first2 + e)
+        elif da:
+            e = (da - 1) * depth + dz
+            push(source, 2, e, place.device(da=da), first3 + e)
+        elif dz:
+            push(source, 3, dz - 1, place.device(dz=dz), first4 + dz - 1)
+    for copy in started:
+        copy.wait_send()
+
+
+def scatter_blocks(a_terms, b_terms):
+    if not kernels_fit():
+        return tuple(
+            lax.psum_scatter(v, ("dp", "fsdp"), scatter_dimension=0, tiled=True)[0].astype(
+                jnp.float32
+            )
+            for v in (a_terms, b_terms)
+        )
+    side, depth = math.isqrt(lax.axis_size("dp")), lax.axis_size("fsdp") // 2
+    half = side * side * depth
+    counts = (half, (side - 1) * side * depth, (side - 1) * depth, depth - 1)
+    vmem = pl.BlockSpec(memory_space=pltpu.VMEM)
+    return pl.pallas_call(
+        functools.partial(scatter_kernel, side, depth),
+        name="scatter_blocks",
+        out_shape=tuple(
+            jax.ShapeDtypeStruct(v.shape[1:], jnp.float32) for v in (a_terms, b_terms)
+        ),
+        in_specs=[vmem] * 2,
+        out_specs=(vmem,) * 2,
+        scratch_shapes=[
+            pltpu.VMEM((max(n, 1),) + v.shape[1:], v.dtype)
+            for v in (a_terms, b_terms)
+            for n in counts
+        ]
+        + [pltpu.SemaphoreType.DMA((2, 2 * half)), pltpu.SemaphoreType.DMA((2, 2 * half))],
+        compiler_params=pltpu.CompilerParams(
+            collective_id=1, has_side_effects=True, vmem_limit_bytes=52 * 2**20
+        ),
+    )(a_terms, b_terms)
 
 
 def shards(
@@ -252,57 +514,55 @@
     share = query_weight.shape[0]
     wide = FF // D
     devices = lax.axis_size("dp") * lax.axis_size("fsdp")
-    used = (4 + 2 * wide) * share + 1
-    rows = round_up(used, 16)
+    start = 4 * D + FF
+
+    def columns(vectors):
+        side_by_side = jnp.concatenate([v.reshape(-1, n) for v, n in vectors], 1).astype(bf16)
+        return jnp.pad(side_by_side, ((0, 0), (0, LANES - side_by_side.shape[1])))
+
     packed = jnp.concatenate(
-        [query_weight, key_weight, value_weight, out_weight]
-        + [inner_weight[:, j * D : (j + 1) * D] for j in range(wide)]
-        + [
-            outer_weight,
-            to_row(
+        [
+            query_weight,
+            key_weight,
+            value_weight,
+            out_weight,
+            inner_weight,
+            columns(
                 [
-                    query_bias,
-                    value_bias,
-                    out_bias,
-                    norm1_gain,
-                    norm1_shift,
-                    outer_bias,
-                    norm2_gain,
-                    norm2_shift,
-                    inner_bias,
-                ],
-                bf16,
+                    (query_bias, 1),
+                    (value_bias, 1),
+                    (out_bias, 1),
+                    (norm1_gain, 1),
+                    (norm1_shift, 1),
+                    (outer_bias, 1),
+                    (norm2_gain, 1),
+                    (norm2_shift, 1),
+                    (inner_bias, wide),
+                ]
             ),
-            jnp.zeros((rows - used, D), bf16),
         ],
-        0,
-    )
-    every = gather_rows(packed)
-
-    def matrix(start, count):
-        return every[:, start * share : (start + count) * share].reshape(-1, D)
-
-    small = every[:, used - 1]
-
-    def vector(start, count=1):
-        return small[:, start * share : (start + count) * share].reshape(-1)
+        1,
+    )
+    every, outer = gather_blocks(packed, outer_weight)
+    every = every.reshape(-1, every.shape[-1])
+    vectors = every[:, start:].T
 
     whole = (
-        matrix(0, 1),
-        vector(0),
-        matrix(1, 1),
-        matrix(2, 1),
-        vector(1),
-        matrix(3, 1),
-        vector(2),
-        vector(3),
-        vector(4),
-        jnp.concatenate([matrix(4 + j, 1) for j in range(wide)], 1),
-        vector(8, wide),
-        matrix(4 + wide, wide),
-        vector(5),
-        vector(6),
-        vector(7),
+        every[:, 0:D],
+        vectors[0],
+        every[:, D : 2 * D],
+        every[:, 2 * D : 3 * D],
+        vectors[1],
+        every[:, 3 * D : 4 * D],
+        vectors[2],
+        vectors[3],
+        vectors[4],
+        every[:, 4 * D : start],
+        vectors[8 : 8 + wide].T.reshape(-1),
+        outer.reshape(FF, D),
+        vectors[5],
+        vectors[6],
+        vectors[7],
     )
     layer_out, saved = forward_pass(tokens, length, whole)
     grad_tokens, sums, factors = backward_pass(tokens, cotangent, length, whole, saved)
@@ -312,12 +572,10 @@
     factor = 1.0 / jnp.sqrt(jnp.float32(tokens.shape[0] * devices))
 
     def weight_block(left, right):
-        block = lax.dot_general(
+        return lax.dot_general(
             left, right, (((0,), (0,)), ((), ())), preferred_element_type=jnp.float32
-        )
-        return block.astype(bf16).reshape(devices, -1, D)
-
-    split = [g.reshape(devices, -1) for g in sums]
+        ).astype(bf16)
+
     order = (0, 1, 2, 3, 4, 6, 7, 8, 5)
     terms = jnp.concatenate(
         [
@@ -325,41 +583,35 @@
             weight_block(tok_rows, d_keys),
             weight_block(tok_rows, d_values),
             weight_block(mixed, d_first_b),
-        ]
-        + [weight_block(hidden_b, d_pre_b[:, j * D : (j + 1) * D]) for j in range(wide)]
-        + [
-            weight_block(act_b, d_second_b),
-            to_row([split[i] for i in order], bf16),
-            jnp.zeros((devices, rows - used, D), bf16),
+            weight_block(hidden_b, d_pre_b),
+            columns([(sums[i], wide if i == 5 else 1) for i in order]),
         ],
         1,
     )
-    owned = scatter_rows(terms) * factor
-
-    def mine(start, count=1):
-        return owned[start * share : (start + count) * share]
-
-    def mine_small(start, count=1):
-        return owned[used - 1, start * share : (start + count) * share]
+    owned, owned_outer = scatter_blocks(
+        terms.reshape(devices, share, -1), weight_block(act_b, d_second_b).reshape(devices, -1, D)
+    )
+    owned = owned * factor
+    owned_vectors = owned[:, start:].T
 
     return (
         layer_out,
         grad_tokens,
-        mine(0),
-        mine_small(0),
-        mine(1),
-        mine(2),
-        mine_small(1),
-        mine(3),
-        mine_small(2),
-        mine_small(3),
-        mine_small(4),
-        jnp.concatenate([mine(4 + j) for j in range(wide)], 1),
-        mine_small(8, wide),
-        mine(4 + wide, wide),
-        mine_small(5),
-        mine_small(6),
-        mine_small(7),
+        owned[:, 0:D],
+        owned_vectors[0],
+        owned[:, D : 2 * D],
+        owned[:, 2 * D : 3 * D],
+        owned_vectors[1],
+        owned[:, 3 * D : 4 * D],
+        owned_vectors[2],
+        owned_vectors[3],
+        owned_vectors[4],
+        owned[:, 4 * D : start],
+        owned_vectors[8 : 8 + wide].T.reshape(-1),
+        owned_outer * factor,
+        owned_vectors[5],
+        owned_vectors[6],
+        owned_vectors[7],
     )
 
 

time: 467 us -> 289 us (0.62)
  waiting for transfers between devices: 269 us -> 0 us
  Pallas kernels: 0 us -> 192 us
  local copies, waits for them, and re-layouts: 132 us -> 43.4 us
  between operations: 15.2 us -> 2.2 us
  matrix products: 40.6 us -> 45.6 us
    pallas_call x0 -> x2, Pallas kernels: none -> 192 us  [the longest x1 111 us: scatter_blocks(): pl.pallas_call(functools.partial(scatter_kernel, side, depth), name='scat...]
    reduce_scatter x1 -> x0, waiting for transfers between devices: 160 us -> none  [scatter_rows(): lax.psum_scatter(blocks, ('dp', 'fsdp'), scatter_dimension=0, tiled=True)]
    all_gather x1 -> x0, waiting for transfers between devices: 108 us -> none  [gather_rows(): return lax.all_gather(block, ('dp', 'fsdp'), axis=0)]
    concatenate x1, local copies, waits for them, and re-layouts: 76 us -> 1.69 us  [shards(): jnp.concatenate([weight_block(tok_rows, d_query), weight_block(tok_rows,...]
    concatenate x3, local copies, waits for them, and re-layouts: 17.7 us -> 2.34 us  [the longest x2 2.32 us: columns(): jnp.concatenate([v.reshape(-1, n) for v, n in vectors], 1).astype(bf16)]
    slice x6 -> x4, local copies, waits for them, and re-layouts: 14.6 us -> 3.21 us  [the longest x1 0.94 us: shards(): vectors = every[:, start:].T]
    reshape x3 -> x19, local copies, waits for them, and re-layouts: 0.73 us -> 10.2 us  [the longest x18 9.59 us: columns(): v.reshape(-1, n)]
    unnamed x83 -> x80, local copies, waits for them, and re-layouts: 5.34 us -> 14.4 us
  transfers between devices with their start and end apart: 2 -> 0, of which waited for: 2 -> 0; matrix products, arithmetic and copies ran while one was open for 1% -> 0% of each run, Pallas kernels for 0% -> 0%
where the time goes in v2:
time: 289 us; the launch traced here: 288 us
  Pallas kernels  192 us (66%)
  matrix products  45.6 us (16%)
  local copies, waits for them, and re-layouts  43.4 us (15%)
  other arithmetic  5.04 us (2%)
    pallas_call x1, Pallas kernels, scatter_blocks(): pl.pallas_call(functools.partial(scatter_kernel, side, depth), name='scat...  111 us
    pallas_call x1, Pallas kernels, gather_blocks(): pl.pallas_call(functools.partial(gather_kernel, side, depth), name='gathe...  81.3 us
    unnamed x80, local copies, waits for them, and re-layouts  14.4 us
    dot_general x6, matrix products, weight_block(): lax.dot_general(left, right, (((0,), (0,)), ((), ())), preferred_element_...  13.3 us
    reshape x18, local copies, waits for them, and re-layouts, columns(): v.reshape(-1, n)  9.59 us
    convert_element_type x4, local copies, waits for them, and re-layouts, weight_block(): return lax.dot_general(left, right, (((0,), (0,)), ((), ())), preferred_e...  8.72 us

profile of v2, /device:TPU:0, one launch (start us, length us, event | category | flops | bytes accessed | tf_op | source)
XLA Modules:
  0.0 288.4 jit_solution(3734326242288085458)
XLA Ops:
  0.7 0.8 constant_dynamic-update-slice_fusion.5
  1.5 0.8 constant_dynamic-update-slice_fusion.4
  2.2 0.8 constant_dynamic-update-slice_fusion.3
  3.0 0.8 constant_dynamic-update-slice_fusion.2
  3.8 0.9 constant_dynamic-update-slice_fusion.1
  4.7 0.7 copy.101
  5.5 0.7 copy.102
  6.2 0.7 copy.103
  7.0 0.7 copy.104
  7.7 0.7 copy.105
  8.4 0.7 copy.106
  9.2 0.7 copy.107
  9.9 0.7 copy.108
  10.7 0.7 reshape.210
  11.6 0.7 copy-done.13
  12.3 81.3 %gather_blocks.1 = (bf16[32,24,6272]{2,1,0:T(8,128)(2,1)}, bf16[32,96,768]{2,1,0:T(8,128)(2,1)}) custom-call(bf16[1,24,6272]{2,1,0:T(8,128)(2,1)} %bitcast.106, bf16[1,96,768]{2,1,0:T(8,128)(2,1)} %bitcast.113), custom_call_target="tpu_custom_call" | custom-call | tf_op jit(solution)/shard_map/gather_blocks/pallas_call | solution.py:344
  93.6 0.9 slice.121
  94.7 0.6 fusion.57
  95.5 0.8 reshape.234
  96.3 1.8 fusion.26
  98.1 1.9 fusion.27
  100.1 2.6 convolution_convert_fusion.9
  104.4 1.7 fusion.76
  106.4 0.8 fusion.6
  107.3 1.0 fusion.77
  108.6 0.8 multiply_reduce_fusion.1
  109.4 1.5 fusion.70
  110.9 2.3 fusion.80
  113.2 2.3 multiply_reduce_fusion.2
  115.5 0.8 fusion.71
  116.3 1.2 convolution_convert_fusion.7
  117.5 1.8 copy.112
  119.3 2.2 fusion.81
  121.5 3.1 %fusion.74 = (bf16[12,64]{1,0:T(8,128)(2,1)}, bf16[128,12,64]{0,2,1:T(8,128)(2,1)}) fusion(bf16[128,12,64]{0,2,1:T(8,128)(2,1)} %bitcast.112, f32[12,128,128]{1,2,0:T(8,128)} %fusion.81, f32[12,128,128]{1,2,0:T(8,128)S(1)} %get-tuple-element.63, f32[12,128]{1,0:T(8,128)S(1)} %log_add_fusion), kind=kOutput, calls=%fused_computation.145 | convolution fusion | flops 26739584 | bytes 1973760 | tf_op jit(solution)/shard_map/hqk,khd->qhd/dot_general | solution.py:174
  124.6 2.7 convolution_add_fusion.2
  127.2 2.5 convolution_convert_fusion.6
  129.7 2.0 convolution_add_fusion.1
  131.7 1.1 fusion.73
  132.8 0.7 copy-done.2
  133.5 2.5 convolution_add_fusion
  136.0 1.5 fusion.13
  137.5 2.4 copy.124
  139.9 2.4 constant_dynamic-update-slice_fusion.9
  142.3 1.5 fusion.14
  143.8 2.4 copy.125
  146.2 2.5 constant_dynamic-update-slice_fusion.8
  148.7 1.5 fusion.15
  150.1 2.4 copy.126
  152.5 2.4 constant_dynamic-update-slice_fusion.7
  155.0 1.5 convolution_convert_fusion.2
  156.5 1.6 copy.127
  158.1 1.2 constant_dynamic-update-slice_fusion.6
  159.5 3.7 %fusion.1 = bf16[768,6272]{1,0:T(8,128)(2,1)} fusion(bf16[768,6272]{1,0:T(8,128)(2,1)} %constant_dynamic-update-slice_fusion.6, bf16[128,3072]{1,0:T(8,128)(2,1)S(1)} %copy-done.9, f32[128,768]{1,0:T(8,128)S(1)} %get-tuple-element.65, f32[768]{0:T(1024)S(1)} %get-tuple-element.36, f32[768]{0:T(1024)S(1)} %get-tuple-element.37, f32[128]{0:T(128)S(1)} %copy-done.28, ...), kind=kOutput, calls=%fused_computation.3 | convolution fusion | flops 606830592 | bytes 5905408 | tf_op jit(solution)/shard_map/dot_general | solution.py:575
  163.6 0.4 reshape.239
  165.1 1.1 reshape.225
  166.2 2.2 concatenate.15
  168.4 1.7 pad_dynamic-update-slice_fusion
  170.1 3.6 %convolution_convert_fusion = bf16[3072,768]{1,0:T(8,128)(2,1)} fusion(f32[128,768]{1,0:T(8,128)S(1)} %copy-done.6, f32[128,3072]{1,0:T(8,128)S(1)} %fusion.6), kind=kOutput, calls=%fused_computation.1 | convolution fusion | flops 608403456 | bytes 6684672 | tf_op jit(solution)/shard_map/dot_general | solution.py:575
  173.8 110.9 %scatter_blocks.1 = (f32[24,6272]{1,0:T(8,128)S(1)}, f32[96,768]{1,0:T(8,128)S(1)}) custom-call(bf16[32,24,6272]{2,1,0:T(8,128)(2,1)} %bitcast.78, bf16[32,96,768]{2,1,0:T(8,128)(2,1)} %bitcast.77), custom_call_target="tpu_custom_call" | custom-call | tf_op jit(solution)/shard_map/scatter_blocks/pallas_call | solution.py:472
  284.7 0.7 fusion.72
  285.4 0.8 slice_reduce_fusion
  286.3 0.7 slice.145
  287.1 0.6 reshape.228
  287.7 0.7 broadcast_multiply_fusion.1
  (98 shorter events, 3.4 us)
Async XLA Ops:
  0.7 95.7 %copy-start.1 = (bf16[128,768]{1,0:T(8,128)(2,1)S(1)}, bf16[128,768]{1,0:T(8,128)(2,1)}, u32[]{:S(2)}) copy-start(bf16[128,768]{1,0:T(8,128)(2,1)} %param.18) | copy-start | bytes 589828
  11.6 0.7 copy-start.13
  98.1 6.1 %copy-start.10 = (bf16[768,128]{1,0:T(8,128)(2,1)}, bf16[768,128]{1,0:T(8,128)(2,1)S(1)}, u32[]{:S(2)}) copy-start(bf16[768,128]{1,0:T(8,128)(2,1)S(1)} %fusion.26) | copy-start | bytes 589828
  98.1 8.3 %copy-start = (bf16[32,24,6272]{2,1,0:T(8,128)(2,1)S(1)}, bf16[32,24,6272]{2,1,0:T(8,128)(2,1)}, u32[]{:S(2)}) copy-start(bf16[32,24,6272]{2,1,0:T(8,128)(2,1)} %get-tuple-element.21) | copy-start | bytes 28901380
  98.1 8.3 %copy-start.22 = (f32[3072]{0:T(1024)S(1)}, f32[3072]{0:T(1024)}, u32[]{:S(2)}) copy-start(f32[3072]{0:T(1024)} %reshape.234) | copy-start | bytes 36868
  100.1 3.9 %copy-start.14 = (bf16[768,128]{1,0:T(8,128)(2,1)}, bf16[768,128]{1,0:T(8,128)(2,1)S(1)}, u32[]{:S(2)}) copy-start(bf16[768,128]{1,0:T(8,128)(2,1)S(1)} %fusion.27) | copy-start | bytes 589828
  100.1 7.2 %slice-start = ((s8[4718592]{0:T(1024)(128)(4,1)}), s8[4194304]{0:T(1024)(128)(4,1)S(1)}, s32[]{:S(2)}) async-start(s8[4718592]{0:T(1024)(128)(4,1)} %bitcast.79), calls=%async_computation | async-start | bytes 8388608
  102.7 1.4 copy-start.15
  106.2 9.4 %copy-start.20 = (f32[128]{0:T(128)}, f32[128]{0:T(128)S(1)}, u32[]{:S(2)}) copy-start(f32[128]{0:T(128)S(1)} %broadcast_multiply_fusion.7) | copy-start | bytes 1540
  106.2 1.1 slice-start.1
  106.4 9.1 %copy-start.27 = (f32[128]{0:T(128)}, f32[128]{0:T(128)S(1)}, u32[]{:S(2)}) copy-start(f32[128]{0:T(128)S(1)} %add_rsqrt_fusion.1) | copy-start | bytes 1540
  106.4 0.9 copy-start.18
  107.3 1.2 copy-start.7
  107.3 1.2 copy-start.16
  107.3 2.0 copy-start.17
  110.9 2.3 copy-start.5
  113.2 2.3 copy-start.8
  129.7 2.0 copy-start.4
  131.7 4.3 %copy-start.12 = (bf16[128,12,64]{0,2,1:T(8,128)(2,1)S(1)}, bf16[128,12,64]{0,2,1:T(8,128)(2,1)}, u32[]{:S(2)}) copy-start(bf16[128,12,64]{0,2,1:T(8,128)(2,1)} %get-tuple-element.61) | copy-start | bytes 589828
  132.8 0.7 copy-start.2
  139.9 2.4 copy-start.11
  146.2 2.5 copy-start.3
  158.1 1.4 copy-start.9
  158.1 1.4 copy-start.21
  158.1 1.4 copy-start.28
  159.5 3.8 %copy-start.30 = (bf16[12,64]{1,0:T(8,128)(2,1)S(1)}, bf16[12,64]{1,0:T(8,128)(2,1)}, u32[]{:S(2)}) copy-start(bf16[12,64]{1,0:T(8,128)(2,1)} %get-tuple-element.60) | copy-start | bytes 4612
  159.5 4.1 %copy-start.19 = (bf16[12,64]{1,0:T(8,128)(2,1)S(1)}, bf16[12,64]{1,0:T(8,128)(2,1)}, u32[]{:S(2)}) copy-start(bf16[12,64]{1,0:T(8,128)(2,1)} %get-tuple-element.58) | copy-start | bytes 4612
  159.5 4.5 %copy-start.26 = (bf16[768]{0:T(1024)(128)(2,1)S(1)}, bf16[768]{0:T(1024)(128)(2,1)}, u32[]{:S(2)}) copy-start(bf16[768]{0:T(1024)(128)(2,1)} %get-tuple-element.51) | copy-start | bytes 4612
  159.5 4.7 %copy-start.32 = (bf16[768]{0:T(1024)(128)(2,1)S(1)}, bf16[768]{0:T(1024)(128)(2,1)}, u32[]{:S(2)}) copy-start(bf16[768]{0:T(1024)(128)(2,1)} %get-tuple-element.27) | copy-start | bytes 4612
  159.5 4.9 %copy-start.31 = (bf16[768]{0:T(1024)(128)(2,1)S(1)}, bf16[768]{0:T(1024)(128)(2,1)}, u32[]{:S(2)}) copy-start(bf16[768]{0:T(1024)(128)(2,1)} %get-tuple-element.32) | copy-start | bytes 4612
  159.5 5.1 %copy-start.25 = (bf16[768]{0:T(1024)(128)(2,1)S(1)}, bf16[768]{0:T(1024)(128)(2,1)}, u32[]{:S(2)}) copy-start(bf16[768]{0:T(1024)(128)(2,1)} %get-tuple-element.49) | copy-start | bytes 4612
  159.5 5.2 %copy-start.24 = (bf16[768]{0:T(1024)(128)(2,1)S(1)}, bf16[768]{0:T(1024)(128)(2,1)}, u32[]{:S(2)}) copy-start(bf16[768]{0:T(1024)(128)(2,1)} %get-tuple-element.25) | copy-start | bytes 4612
  159.5 5.4 %copy-start.23 = (bf16[768]{0:T(1024)(128)(2,1)S(1)}, bf16[768]{0:T(1024)(128)(2,1)}, u32[]{:S(2)}) copy-start(bf16[768]{0:T(1024)(128)(2,1)} %get-tuple-element.31) | copy-start | bytes 4612
  163.2 1.9 copy-start.29
  164.6 5.6 %copy-start.6 = (f32[128,768]{1,0:T(8,128)S(1)}, f32[128,768]{1,0:T(8,128)}, u32[]{:S(2)}) copy-start(f32[128,768]{1,0:T(8,128)} %copy-done.5) | copy-start | bytes 1179652

commit v3 on v2

--- a/solution.py
+++ b/solution.py
@@ -249,7 +249,7 @@
         return self.column(a, b, c) * (2 * self.depth) + z * 2 + c
 
 
-def meet(place):
+def greet(place):
     barrier = pltpu.get_barrier_semaphore()
     others = [place.device(da=k) for k in range(1, place.side)]
     others += [place.device(db=k) for k in range(1, place.side)]
@@ -257,12 +257,19 @@
     others.append(place.sibling())
     for other in others:
         pl.semaphore_signal(barrier, inc=1, device_id=other, device_id_type=MESH)
-    pl.semaphore_wait(barrier, len(others))
-
-
-def gather_kernel(side, depth, a_ref, b_ref, a_out, b_out, keep, sent, got):
+    return len(others)
+
+
+def gather_kernel(side, depth, parts, *refs):
+    part_refs = refs[:parts]
+    b_ref, a_out, b_out, a_ref, keep, sent, got = refs[parts:]
     place = Place(side, depth)
-    meet(place)
+    greeted = greet(place)
+    at = 0
+    for part in part_refs:
+        a_ref[0, :, at : at + part.shape[1]] = part[...]
+        at += part.shape[1]
+    pl.semaphore_wait(pltpu.get_barrier_semaphore(), greeted)
     pairs = ((a_ref, a_out), (b_ref, b_out))
     me = place.block(0, 0, 0)
     own = [
@@ -335,34 +342,69 @@
     return side * side == lax.axis_size("dp") and lax.axis_size("fsdp") % 2 == 0 and devices <= 32
 
 
-def gather_blocks(a_block, b_block):
+def gather_blocks(a_parts, b_block):
     if not kernels_fit():
+        a_block = jnp.concatenate(a_parts, 1)
         return tuple(lax.all_gather(v, ("dp", "fsdp"), axis=0) for v in (a_block, b_block))
     side, depth = math.isqrt(lax.axis_size("dp")), lax.axis_size("fsdp") // 2
     devices = 2 * side * side * depth
+    rows, lanes = b_block.shape[0], sum(v.shape[1] for v in a_parts)
+    share = a_parts[0].shape[0]
+    dtype = b_block.dtype
     anywhere = pl.BlockSpec(memory_space=pl.ANY)
+    vmem = pl.BlockSpec(memory_space=pltpu.VMEM)
     return pl.pallas_call(
-        functools.partial(gather_kernel, side, depth),
+        functools.partial(gather_kernel, side, depth, len(a_parts)),
         name="gather_blocks",
-        out_shape=tuple(
-            jax.ShapeDtypeStruct((devices,) + v.shape, v.dtype) for v in (a_block, b_block)
+        out_shape=(
+            jax.ShapeDtypeStruct((devices, share, lanes), dtype),
+            jax.ShapeDtypeStruct((devices, rows, D), dtype),
         ),
-        in_specs=[anywhere] * 2,
+        in_specs=[vmem] * len(a_parts) + [anywhere],
         out_specs=(anywhere,) * 2,
         scratch_shapes=[
+            pltpu.VMEM((1, share, lanes), dtype),
             pltpu.SemaphoreType.DMA((2,)),
             pltpu.SemaphoreType.DMA((2, devices)),
             pltpu.SemaphoreType.DMA((2, devices)),
         ],
         compiler_params=pltpu.CompilerParams(collective_id=0, has_side_effects=True),
-    )(a_block[None], b_block[None])
-
-
-def scatter_kernel(side, depth, a_in, b_in, a_out, b_out, *scratch):
-    a_bufs, b_bufs = scratch[0:4], scratch[4:8]
-    sent, got = scratch[8:10]
+    )(*a_parts, b_block[None])
+
+
+def product(left, right):
+    return lax.dot_general(
+        left, right, (((0,), (0,)), ((), ())), preferred_element_type=jnp.float32
+    )
+
+
+def fill(factors, column_ref, a_in, b_in):
+    tok, d_query, d_keys, d_values, mixed, d_first, hidden, d_pre, act, d_second = factors
+    share, outer_share = a_in.shape[1], b_in.shape[1]
+    part = D // 2
+    pairs = [(tok, d_query, 0), (tok, d_keys, 0), (tok, d_values, 0), (mixed, d_first, 0)]
+    pairs += [(hidden, d_pre, j * D) for j in range(FF // D)]
+    for at, (left, right, lane) in enumerate(pairs):
+        for m in range(0, D, part):
+            block = product(left[:, m : m + part], right[:, lane : lane + D])
+            block = block.reshape(part // share, share, D).astype(jnp.bfloat16)
+            a_in[m // share : (m + part) // share, :, at * D : (at + 1) * D] = block
+    a_in[:, :, len(pairs) * D :] = column_ref[...]
+    for m in range(0, FF, part):
+        block = product(act[:, m : m + part], d_second[...])
+        block = block.reshape(part // outer_share, outer_share, D).astype(jnp.bfloat16)
+        b_in[m // outer_share : (m + part) // outer_share] = block
+
+
+def scatter_kernel(side, depth, *refs):
+    factors, column_ref, a_out, b_out = refs[0:10], refs[10], refs[11], refs[12]
+    a_in, b_in = refs[13:15]
+    a_bufs, b_bufs = refs[15:19], refs[19:23]
+    sent, got = refs[23:25]
     place = Place(side, depth)
-    meet(place)
+    greeted = greet(place)
+    fill(factors, column_ref, a_in, b_in)
+    pl.semaphore_wait(pltpu.get_barrier_semaphore(), greeted)
     started = []
     half = side * side * depth
     first2 = half
@@ -457,8 +499,16 @@
         copy.wait_send()
 
 
-def scatter_blocks(a_terms, b_terms):
+def scatter_blocks(factors, column_terms):
+    devices = lax.axis_size("dp") * lax.axis_size("fsdp")
+    share, outer_share = D // devices, FF // devices
+    bf16 = jnp.bfloat16
     if not kernels_fit():
+        tok, d_query, d_keys, d_values, mixed, d_first, hidden, d_pre, act, d_second = factors
+        pairs = ((tok, d_query), (tok, d_keys), (tok, d_values), (mixed, d_first), (hidden, d_pre))
+        a_terms = [product(left, right).astype(bf16) for left, right in pairs]
+        a_terms = jnp.concatenate(a_terms + [column_terms], 1).reshape(devices, share, -1)
+        b_terms = product(act, d_second).astype(bf16).reshape(devices, outer_share, D)
         return tuple(
             lax.psum_scatter(v, ("dp", "fsdp"), scatter_dimension=0, tiled=True)[0].astype(
                 jnp.float32
@@ -469,24 +519,20 @@
     half = side * side * depth
     counts = (half, (side - 1) * side * depth, (side - 1) * depth, depth - 1)
     vmem = pl.BlockSpec(memory_space=pltpu.VMEM)
+    shapes = ((share, 4 * D + FF + LANES), (outer_share, D))
     return pl.pallas_call(
         functools.partial(scatter_kernel, side, depth),
         name="scatter_blocks",
-        out_shape=tuple(
-            jax.ShapeDtypeStruct(v.shape[1:], jnp.float32) for v in (a_terms, b_terms)
-        ),
-        in_specs=[vmem] * 2,
+        out_shape=tuple(jax.ShapeDtypeStruct(v, jnp.float32) for v in shapes),
+        in_specs=[vmem] * 11,
         out_specs=(vmem,) * 2,
-        scratch_shapes=[
-            pltpu.VMEM((max(n, 1),) + v.shape[1:], v.dtype)
-            for v in (a_terms, b_terms)
-            for n in counts
-        ]
-        + [pltpu.SemaphoreType.DMA((2, 2 * half)), pltpu.SemaphoreType.DMA((2, 2 * half))],
+        scratch_shapes=[pltpu.VMEM((devices,) + v, bf16) for v in shapes]
+        + [pltpu.VMEM((max(n, 1),) + v, bf16) for v in shapes for n in counts]
+        + [pltpu.SemaphoreType.DMA((2, devices)), pltpu.SemaphoreType.DMA((2, devices))],
         compiler_params=pltpu.CompilerParams(
             collective_id=1, has_side_effects=True, vmem_limit_bytes=52 * 2**20
         ),
-    )(a_terms, b_terms)
+    )(*factors, column_terms.reshape(devices, share, LANES))
 
 
 def shards(
@@ -516,34 +562,29 @@
     devices = lax.axis_size("dp") * lax.axis_size("fsdp")
     start = 4 * D + FF
 
-    def columns(vectors):
-        side_by_side = jnp.concatenate([v.reshape(-1, n) for v, n in vectors], 1).astype(bf16)
-        return jnp.pad(side_by_side, ((0, 0), (0, LANES - side_by_side.shape[1])))
-
-    packed = jnp.concatenate(
+    def columns(vectors, long_one):
+        flat = jnp.concatenate(list(vectors) + [long_one.reshape(-1, wide).T.reshape(-1)])
+        side_by_side = flat.reshape(len(vectors) + wide, -1)
+        padding = LANES - side_by_side.shape[0]
+        return jnp.pad(side_by_side.astype(bf16), ((0, padding), (0, 0))).T
+
+    vector_block = columns(
         [
-            query_weight,
-            key_weight,
-            value_weight,
-            out_weight,
-            inner_weight,
-            columns(
-                [
-                    (query_bias, 1),
-                    (value_bias, 1),
-                    (out_bias, 1),
-                    (norm1_gain, 1),
-                    (norm1_shift, 1),
-                    (outer_bias, 1),
-                    (norm2_gain, 1),
-                    (norm2_shift, 1),
-                    (inner_bias, wide),
-                ]
-            ),
+            query_bias,
+            value_bias,
+            out_bias,
+            norm1_gain,
+            norm1_shift,
+            outer_bias,
+            norm2_gain,
+            norm2_shift,
         ],
-        1,
-    )
-    every, outer = gather_blocks(packed, outer_weight)
+        inner_bias,
+    )
+    every, outer = gather_blocks(
+        [query_weight, key_weight, value_weight, out_weight, inner_weight, vector_block],
+        outer_weight,
+    )
     every = every.reshape(-1, every.shape[-1])
     vectors = every[:, start:].T
 
@@ -566,31 +607,9 @@
     )
     layer_out, saved = forward_pass(tokens, length, whole)
     grad_tokens, sums, factors = backward_pass(tokens, cotangent, length, whole, saved)
-    tok_rows, d_query, d_keys, d_values, mixed, d_first_b, hidden_b, d_pre_b, act_b, d_second_b = (
-        factors
-    )
     factor = 1.0 / jnp.sqrt(jnp.float32(tokens.shape[0] * devices))
-
-    def weight_block(left, right):
-        return lax.dot_general(
-            left, right, (((0,), (0,)), ((), ())), preferred_element_type=jnp.float32
-        ).astype(bf16)
-
-    order = (0, 1, 2, 3, 4, 6, 7, 8, 5)
-    terms = jnp.concatenate(
-        [
-            weight_block(tok_rows, d_query),
-            weight_block(tok_rows, d_keys),
-            weight_block(tok_rows, d_values),
-            weight_block(mixed, d_first_b),
-            weight_block(hidden_b, d_pre_b),
-            columns([(sums[i], wide if i == 5 else 1) for i in order]),
-        ],
-        1,
-    )
-    owned, owned_outer = scatter_blocks(
-        terms.reshape(devices, share, -1), weight_block(act_b, d_second_b).reshape(devices, -1, D)
-    )
+    column_terms = columns([sums[i] for i in (0, 1, 2, 3, 4, 6, 7, 8)], sums[5])
+    owned, owned_outer = scatter_blocks(factors, column_terms)
     owned = owned * factor
     owned_vectors = owned[:, start:].T
 

time: 289 us -> 254 us (0.88)
  local copies, waits for them, and re-layouts: 43.4 us -> 22.2 us
  matrix products: 45.6 us -> 33.8 us
    dot_general x6 -> x0, matrix products: 13.3 us -> none  [weight_block(): lax.dot_general(left, right, (((0,), (0,)), ((), ())), preferred_element_...]
    unnamed x80 -> x33, local copies, waits for them, and re-layouts: 14.4 us -> 5.13 us
    reshape x18 -> x6, local copies, waits for them, and re-layouts: 9.59 us -> 2.15 us  [the longest x4 1.97 us: columns(): long_one.reshape(-1, wide).T.reshape(-1)]
    convert_element_type x4 -> x5, local copies, waits for them, and re-layouts: 8.72 us -> 1.96 us  [the longest x1 1.37 us: columns(): return jnp.pad(side_by_side.astype(bf16), ((0, padding), (0, 0))).T]
    pallas_call x1, Pallas kernels: 111 us -> 108 us  [scatter_blocks(): pl.pallas_call(functools.partial(scatter_kernel, side, depth), name='scat...]
    concatenate x4 -> x2, local copies, waits for them, and re-layouts: 4.02 us -> 6.06 us  [columns(): jnp.concatenate(list(vectors) + [long_one.reshape(-1, wide).T.reshape(-1)])]
where the time goes in v3:
time: 254 us; the launch traced here: 253 us
  Pallas kernels  190 us (75%)
  matrix products  33.8 us (13%)
  local copies, waits for them, and re-layouts  22.2 us (9%)
  other arithmetic  5.24 us (2%)
    pallas_call x1, Pallas kernels, scatter_blocks(): pl.pallas_call(functools.partial(scatter_kernel, side, depth), name='scat...  108 us
    pallas_call x1, Pallas kernels, gather_blocks(): pl.pallas_call(functools.partial(gather_kernel, side, depth, len(a_parts)...  82 us
    concatenate x2, local copies, waits for them, and re-layouts, columns(): jnp.concatenate(list(vectors) + [long_one.reshape(-1, wide).T.reshape(-1)])  6.06 us
    unnamed x33, local copies, waits for them, and re-layouts  5.13 us

profile of v3, /device:TPU:0, one launch (start us, length us, event | category | flops | bytes accessed | tf_op | source)
XLA Modules:
  0.0 253.1 jit_solution(18056076430925613799)
XLA Ops:
  0.7 0.7 reshape.155
  1.4 0.1 copy.46
  1.6 5.4 %concatenate.7 = bf16[288]{0:T(512)(128)(2,1)S(1)} concatenate(bf16[24]{0:T(256)(128)(2,1)} %param.22, bf16[24]{0:T(256)(128)(2,1)} %param.25, bf16[24]{0:T(256)(128)(2,1)} %param.27, bf16[24]{0:T(256)(128)(2,1)} %param.28, bf16[24]{0:T(256)(128)(2,1)} %param.29, bf16[24]{0:T(256)(128)(2,1)} %param.33, bf16[24]{0:T(256)(128)(2,1)} %param.34, bf16[24]{0:T(256)(128)(2,1)} %param.35, ...), dimensions={0} | concatenate | bytes 1152 | tf_op jit(solution)/shard_map/concatenate | solution.py:566
  7.0 0.1 reshape.157
  7.1 0.1 copy.47
  7.2 0.6 pad_bitcast_fusion.1.refs_5_
  7.8 82.0 %gather_blocks.1 = (bf16[32,24,6272]{2,1,0:T(8,128)(2,1)}, bf16[32,96,768]{2,1,0:T(8,128)(2,1)}) custom-call(bf16[24,768]{1,0:T(8,128)(2,1)} %refs_0_.2, bf16[24,768]{1,0:T(8,128)(2,1)} %refs_1_.1, bf16[24,768]{1,0:T(8,128)(2,1)} %refs_2_.1, bf16[24,768]{1,0:T(8,128)(2,1)} %refs_3_.1, bf16[24,3072]{1,0:T(8,128)(2,1)} %refs_4_.1, ...), custom_call_target="tpu_custom_call" | custom-call | tf_op jit(solution)/shard_map/gather_blocks/pallas_call | solution.py:356
  89.9 1.0 slice.121
  90.9 0.1 copy.65
  91.1 1.8 fusion.23
  92.9 1.9 convolution_convert_fusion.3
  95.5 0.3 fusion.64
  95.8 0.1 exponential_reduce_fusion
  96.0 1.8 fusion.22
  97.8 0.2 convolution_convert_fusion.2
  98.0 1.7 fusion.65
  99.7 0.2 multiply_reduce_fusion.6
  100.0 0.1 fusion.43.refs_6_
  100.1 0.2 copy.50
  100.3 0.2 reshape.173
  100.5 3.0 %multiply_convert_fusion = (bf16[128,3072]{1,0:T(8,128)(2,1)S(1)}, f32[128,3072]{1,0:T(8,128)S(1)}) fusion(f32[3072]{0:T(1024)S(1)} %reshape.173, bf16[128,768]{1,0:T(8,128)(2,1)S(1)} %fusion.43.refs_6_, bf16[768,6272]{1,0:T(8,128)(2,1)} %bitcast.73), kind=kOutput, calls=%fused_computation.12 | convolution fusion | flops 606339072 | bytes 7286784 | tf_op jit(solution)/shard_map/dot_general | solution.py:98
  103.6 3.6 %fusion.66 = (f32[128]{0:T(128)S(1)}, f32[128,768]{1,0:T(8,128)S(1)}) fusion(f32[768]{0:T(1024)S(1)} %get-tuple-element.35, bf16[128,3072]{1,0:T(8,128)(2,1)S(1)} %get-tuple-element.68.refs_8_, bf16[3072,768]{1,0:T(8,128)(2,1)} %bitcast.64, f32[768]{0:T(1024)S(1)} %get-tuple-element.36, f32[768]{0:T(1024)S(1)} %get-tuple-element.37, ...), kind=kOutput, calls=%fused_computation.125 | convolution fusion | flops 604667776 | bytes 6302208 | tf_op jit(solution)/shard_map/dot_general | solution.py:102
  107.2 0.2 multiply_reduce_fusion.5
  107.4 0.2 multiply_reduce_fusion.1
  107.6 1.5 fusion.58
  109.2 2.3 fusion.60
  111.5 5.0 %multiply_reduce_fusion.2 = (bf16[768]{0:T(1024)(128)(2,1)}, f32[128]{0:T(128)S(1)}, f32[128]{0:T(128)S(1)}, bf16[768]{0:T(1024)(128)(2,1)}, f32[128,768]{1,0:T(8,128)S(1)}) fusion(f32[128,768]{1,0:T(8,128)S(1)} %get-tuple-element.67, f32[128]{0:T(128)S(1)} %add_rsqrt_fusion.1, f32[128]{0:T(128)S(1)} %broadcast_multiply_fusion.7, ...), kind=kOutput, calls=%fused_computation.53 | convolution fusion | flops 604961024 | bytes 6692864 | tf_op jit(solution)/shard_map/dot_general | solution.py:160
  116.6 0.8 fusion.59
  117.4 1.8 convolution_convert_fusion.1
  119.2 0.2 copy.51
  119.3 0.5 fusion.62
  119.8 0.6 reduce_sum.188
  120.4 0.3 fusion.69
  120.8 1.6 fusion.63
  122.5 0.2 dynamic-update-slice
  122.7 0.2 dynamic-update-slice.1
  122.9 0.9 dynamic-update-slice.2
  123.7 0.9 dynamic-update-slice.3
  124.6 0.9 dynamic-update-slice.4
  125.5 0.8 dynamic-update-slice.5
  126.3 0.2 dynamic-update-slice.6
  126.5 0.3 dynamic-update-slice.7
  126.9 0.6 copy-done.8
  127.5 1.1 reshape.164
  128.6 0.1 copy.55
  128.7 0.6 constant_dynamic-update-slice_fusion
  129.3 1.4 convert_element_type.137
  130.7 0.8 pad_bitcast_fusion
  131.4 0.2 copy.56
  131.6 0.2 copy.59.refs_3_
  131.8 1.8 convolution_convert_fusion
  133.6 0.1 copy.58.refs_2_
  133.7 0.1 copy.57.refs_1_
  133.9 0.1 copy.60.refs_4_
  134.0 108.0 %scatter_blocks.1 = (f32[24,6272]{1,0:T(8,128)}, f32[96,768]{1,0:T(8,128)}) custom-call(bf16[128,768]{1,0:T(8,128)(2,1)S(1)} %copy-done, bf16[128,768]{1,0:T(8,128)(2,1)S(1)} %copy.57.refs_1_, bf16[128,768]{1,0:T(8,128)(2,1)S(1)} %copy.58.refs_2_, bf16[128,768]{1,0:T(8,128)(2,1)S(1)} %copy.59.refs_3_, bf16[128,768]{1,0:T(8,128)(2,1)S(1)} %copy.60.refs_4_, ...), custom_call_target="tpu_custom_call" | custom-call | tf_op jit(solution)/shard_map/scatter_blocks/pallas_call | solution.py:523
  242.1 1.2 broadcast_multiply_fusion
  243.2 0.7 fusion.61
  243.9 0.7 slice.145
  244.7 0.6 reshape.167
  245.3 0.8 slice_reduce_fusion
  246.2 0.7 broadcast_multiply_fusion.1
  246.9 1.8 convolution_add_fusion.2
  248.7 1.8 convolution_add_fusion.1
  250.5 2.6 %convolution_add_fusion = f32[128,768]{1,0:T(8,128)} fusion(f32[128,768]{1,0:T(8,128)S(1)} %convolution_add_fusion.1, bf16[128,768]{0,1:T(8,128)(2,1)S(1)} %bitcast.82, bf16[768,6272]{1,0:T(8,128)(2,1)} %bitcast.78), kind=kOutput, calls=%fused_computation.20 | convolution fusion | flops 151093248 | bytes 2162688 | tf_op jit(solution)/shard_map/dot_general | solution.py:187
  (43 shorter events, 0.5 us)
Async XLA Ops:
  89.9 3.0 %copy-start = (bf16[128,768]{1,0:T(8,128)(2,1)S(1)}, bf16[128,768]{1,0:T(8,128)(2,1)}, u32[]{:S(2)}) copy-start(bf16[128,768]{1,0:T(8,128)(2,1)} %refs_0_.3) | copy-start | bytes 589828
  92.9 2.9 %copy-start.6 = (bf16[768,128]{1,0:T(8,128)(2,1)}, bf16[768,128]{1,0:T(8,128)(2,1)S(1)}, u32[]{:S(2)}) copy-start(bf16[768,128]{1,0:T(8,128)(2,1)S(1)} %fusion.23) | copy-start | bytes 589828
  94.8 3.0 %copy-start.7 = (bf16[768,128]{1,0:T(8,128)(2,1)}, bf16[768,128]{1,0:T(8,128)(2,1)S(1)}, u32[]{:S(2)}) copy-start(bf16[768,128]{1,0:T(8,128)(2,1)S(1)} %convolution_convert_fusion.3) | copy-start | bytes 589828
  103.5 3.6 %copy-start.1 = (bf16[128,3072]{1,0:T(8,128)(2,1)}, bf16[128,3072]{1,0:T(8,128)(2,1)S(1)}, u32[]{:S(2)}) copy-start(bf16[128,3072]{1,0:T(8,128)(2,1)S(1)} %get-tuple-element.68.refs_8_) | copy-start | bytes 2359300
  103.5 5.6 %slice-start = ((s8[4718592]{0:T(1024)(128)(4,1)}), s8[4194304]{0:T(1024)(128)(4,1)S(1)}, s32[]{:S(2)}) async-start(s8[4718592]{0:T(1024)(128)(4,1)} %bitcast.65), calls=%async_computation | async-start | bytes 8388608
  103.6 3.8 %copy-start.2 = (f32[128,768]{1,0:T(8,128)S(1)}, f32[128,768]{1,0:T(8,128)}, u32[]{:S(2)}) copy-start(f32[128,768]{1,0:T(8,128)} %param.20) | copy-start | bytes 1179652
  103.6 5.6 %slice-start.1 = ((s8[4718592]{0:T(1024)(128)(4,1)}), s8[524288]{0:T(1024)(128)(4,1)S(1)}, s32[]{:S(2)}) async-start(s8[4718592]{0:T(1024)(128)(4,1)} %bitcast.65), calls=%async_computation.1 | async-start | bytes 1048576
  111.5 5.0 %copy-start.4 = (bf16[128,3072]{1,0:T(8,128)(2,1)}, bf16[128,3072]{1,0:T(8,128)(2,1)S(1)}, u32[]{:S(2)}) copy-start(bf16[128,3072]{1,0:T(8,128)(2,1)S(1)} %get-tuple-element.54.refs_7_) | copy-start | bytes 2359300
  120.8 9.9 %copy-start.3 = (f32[12,128,128]{1,2,0:T(8,128)}, f32[12,128,128]{1,2,0:T(8,128)S(1)}, u32[]{:S(2)}) copy-start(f32[12,128,128]{1,2,0:T(8,128)S(1)} %fusion.69) | copy-start | bytes 2359300
  120.8 1.9 copy-start.9
  126.8 0.6 copy-start.8
  242.0 4.1 %copy-start.5 = (f32[96,768]{1,0:T(8,128)S(1)}, f32[96,768]{1,0:T(8,128)}, u32[]{:S(2)}) copy-start(f32[96,768]{1,0:T(8,128)} %get-tuple-element.24) | copy-start | bytes 884740

commit v4 on v3

--- a/solution.py
+++ b/solution.py
@@ -279,42 +279,45 @@
     for copy in own:
         copy.start()
     started = []
+    counts = [0, 0]
     half = side * side * depth
 
     def slot(da, db, dz):
         return (db * side + da) * depth + dz
 
-    def push(source, device, at, index, sem_at):
-        for i, (src, dst) in enumerate(pairs):
+    def push(piece, source, device, at, sem_at):
+        for i, (src, dst) in [(piece, pairs[piece])]:
             origin = src.at[0] if source is None else dst.at[source]
             copy = pltpu.make_async_remote_copy(
                 src_ref=origin,
                 dst_ref=dst.at[at],
-                send_sem=sent.at[i, len(started) // 2],
+                send_sem=sent.at[i, counts[i]],
                 recv_sem=got.at[i, sem_at],
                 device_id=device,
                 device_id_type=MESH,
             )
             copy.start()
+            counts[i] += 1
             started.append(copy)
 
-    def landed(index, sem_at):
-        for i, (src, dst) in enumerate(pairs):
-            pltpu.make_async_copy(dst.at[index], dst.at[index], got.at[i, sem_at]).wait()
-
-    def spread(source, da, db, dz):
+    def landed(piece, index, sem_at):
+        dst = pairs[piece][1]
+        pltpu.make_async_copy(dst.at[index], dst.at[index], got.at[piece, sem_at]).wait()
+
+    def spread(piece, source, da, db, dz):
         index = place.block(da, db, dz)
         if da == 0 and db == 0:
             for k in range(1, side):
-                push(source, place.device(da=k), index, index, slot((side - k) % side, 0, dz))
+                push(piece, source, place.device(da=k), index, slot((side - k) % side, 0, dz))
         if db == 0:
             for k in range(1, side):
-                push(source, place.device(db=k), index, index, slot(da, (side - k) % side, dz))
-        push(source, place.sibling(), index, index, half + slot(da, db, dz))
-
-    for dz in range(1, depth):
-        push(None, place.device(dz=dz), me, me, slot(0, 0, depth - dz))
-    spread(None, 0, 0, 0)
+                push(piece, source, place.device(db=k), index, slot(da, (side - k) % side, dz))
+        push(piece, source, place.sibling(), index, half + slot(da, db, dz))
+
+    for piece in range(2):
+        for dz in range(1, depth):
+            push(piece, None, place.device(dz=dz), me, slot(0, 0, depth - dz))
+        spread(piece, None, 0, 0, 0)
     near = sorted(range(1, depth), key=lambda k: min(k, depth - k))
     steps = []
     for rank, dz in enumerate([0] + near):
@@ -324,12 +327,14 @@
                     steps.append((rank + (da > 0) + 2 * (db > 0), da, db, dz))
     for _, da, db, dz in sorted(steps):
         index = place.block(da, db, dz)
-        landed(index, slot(da, db, dz))
-        spread(index, da, db, dz)
+        for piece in range(2):
+            landed(piece, index, slot(da, db, dz))
+            spread(piece, index, da, db, dz)
     for db in range(side):
         for da in range(side):
             for dz in range(depth):
-                landed(place.sibling_block(da, db, dz), half + slot(da, db, dz))
+                for piece in range(2):
+                    landed(piece, place.sibling_block(da, db, dz), half + slot(da, db, dz))
     for copy in own:
         copy.wait()
     for copy in started:

time: 254 us -> 247 us (0.972)
  Pallas kernels: 190 us -> 183 us
    pallas_call x1, Pallas kernels: 108 us -> 104 us  [scatter_blocks(): pl.pallas_call(functools.partial(scatter_kernel, side, depth), name='scat...]
where the time goes in v4:
time: 247 us; the launch traced here: 246 us
  Pallas kernels  183 us (74%)
  matrix products  33.8 us (14%)
  local copies, waits for them, and re-layouts  22.2 us (9%)
  other arithmetic  5.24 us (2%)
    pallas_call x1, Pallas kernels, scatter_blocks(): pl.pallas_call(functools.partial(scatter_kernel, side, depth), name='scat...  104 us
    pallas_call x1, Pallas kernels, gather_blocks(): pl.pallas_call(functools.partial(gather_kernel, side, depth, len(a_parts)...  79.7 us
    concatenate x2, local copies, waits for them, and re-layouts, columns(): jnp.concatenate(list(vectors) + [long_one.reshape(-1, wide).T.reshape(-1)])  6.06 us
    unnamed x33, local copies, waits for them, and re-layouts  5.13 us
    dot_general x1, matrix products, backward_pass(): jnp.dot(d_pre_b, inner_weight.T, preferred_element_type=f32)  5.01 us

profile of v4, /device:TPU:0, one launch (start us, length us, event | category | flops | bytes accessed | tf_op | source)
XLA Modules:
  0.0 246.4 jit_solution(15976601275323485747)
XLA Ops:
  0.7 0.7 reshape.155
  1.4 0.1 copy.46
  1.6 5.4 %concatenate.7 = bf16[288]{0:T(512)(128)(2,1)S(1)} concatenate(bf16[24]{0:T(256)(128)(2,1)} %param.22, bf16[24]{0:T(256)(128)(2,1)} %param.25, bf16[24]{0:T(256)(128)(2,1)} %param.27, bf16[24]{0:T(256)(128)(2,1)} %param.28, bf16[24]{0:T(256)(128)(2,1)} %param.29, bf16[24]{0:T(256)(128)(2,1)} %param.33, bf16[24]{0:T(256)(128)(2,1)} %param.34, bf16[24]{0:T(256)(128)(2,1)} %param.35, ...), dimensions={0} | concatenate | bytes 1152 | tf_op jit(solution)/shard_map/concatenate | solution.py:571
  7.0 0.1 reshape.157
  7.1 0.1 copy.47
  7.2 0.6 pad_bitcast_fusion.1.refs_5_
  7.8 79.7 %gather_blocks.1 = (bf16[32,24,6272]{2,1,0:T(8,128)(2,1)}, bf16[32,96,768]{2,1,0:T(8,128)(2,1)}) custom-call(bf16[24,768]{1,0:T(8,128)(2,1)} %refs_0_.2, bf16[24,768]{1,0:T(8,128)(2,1)} %refs_1_.1, bf16[24,768]{1,0:T(8,128)(2,1)} %refs_2_.1, bf16[24,768]{1,0:T(8,128)(2,1)} %refs_3_.1, bf16[24,3072]{1,0:T(8,128)(2,1)} %refs_4_.1, ...), custom_call_target="tpu_custom_call" | custom-call | tf_op jit(solution)/shard_map/gather_blocks/pallas_call | solution.py:361
  87.5 1.0 slice.121
  88.5 0.1 copy.65
  88.8 1.8 fusion.23
  90.6 1.9 convolution_convert_fusion.3
  93.1 0.3 fusion.64
  93.5 0.1 exponential_reduce_fusion
  93.6 1.8 fusion.22
  95.4 0.2 convolution_convert_fusion.2
  95.7 1.7 fusion.65
  97.4 0.2 multiply_reduce_fusion.6
  97.6 0.1 fusion.43.refs_6_
  97.8 0.2 copy.50
  97.9 0.2 reshape.173
  98.2 3.0 %multiply_convert_fusion = (bf16[128,3072]{1,0:T(8,128)(2,1)S(1)}, f32[128,3072]{1,0:T(8,128)S(1)}) fusion(f32[3072]{0:T(1024)S(1)} %reshape.173, bf16[128,768]{1,0:T(8,128)(2,1)S(1)} %fusion.43.refs_6_, bf16[768,6272]{1,0:T(8,128)(2,1)} %bitcast.73), kind=kOutput, calls=%fused_computation.12 | convolution fusion | flops 606339072 | bytes 7286784 | tf_op jit(solution)/shard_map/dot_general | solution.py:98
  101.2 3.6 %fusion.66 = (f32[128]{0:T(128)S(1)}, f32[128,768]{1,0:T(8,128)S(1)}) fusion(f32[768]{0:T(1024)S(1)} %get-tuple-element.35, bf16[128,3072]{1,0:T(8,128)(2,1)S(1)} %get-tuple-element.68.refs_8_, bf16[3072,768]{1,0:T(8,128)(2,1)} %bitcast.64, f32[768]{0:T(1024)S(1)} %get-tuple-element.36, f32[768]{0:T(1024)S(1)} %get-tuple-element.37, ...), kind=kOutput, calls=%fused_computation.125 | convolution fusion | flops 604667776 | bytes 6302208 | tf_op jit(solution)/shard_map/dot_general | solution.py:102
  104.8 0.2 multiply_reduce_fusion.5
  105.0 0.2 multiply_reduce_fusion.1
  105.3 1.5 fusion.58
  106.8 2.3 fusion.60
  109.2 5.0 %multiply_reduce_fusion.2 = (bf16[768]{0:T(1024)(128)(2,1)}, f32[128]{0:T(128)S(1)}, f32[128]{0:T(128)S(1)}, bf16[768]{0:T(1024)(128)(2,1)}, f32[128,768]{1,0:T(8,128)S(1)}) fusion(f32[128,768]{1,0:T(8,128)S(1)} %get-tuple-element.67, f32[128]{0:T(128)S(1)} %add_rsqrt_fusion.1, f32[128]{0:T(128)S(1)} %broadcast_multiply_fusion.7, ...), kind=kOutput, calls=%fused_computation.53 | convolution fusion | flops 604961024 | bytes 6692864 | tf_op jit(solution)/shard_map/dot_general | solution.py:160
  114.2 0.8 fusion.59
  115.0 1.8 convolution_convert_fusion.1
  116.8 0.2 copy.51
  117.0 0.5 fusion.62
  117.5 0.6 reduce_sum.188
  118.1 0.3 fusion.69
  118.4 1.6 fusion.63
  120.1 0.2 dynamic-update-slice
  120.3 0.2 dynamic-update-slice.1
  120.5 0.9 dynamic-update-slice.2
  121.4 0.9 dynamic-update-slice.3
  122.2 0.9 dynamic-update-slice.4
  123.1 0.8 dynamic-update-slice.5
  123.9 0.2 dynamic-update-slice.6
  124.1 0.3 dynamic-update-slice.7
  124.5 0.6 copy-done.8
  125.1 1.1 reshape.164
  126.2 0.1 copy.55
  126.3 0.6 constant_dynamic-update-slice_fusion
  127.0 1.4 convert_element_type.137
  128.3 0.8 pad_bitcast_fusion
  129.1 0.2 copy.56
  129.2 0.2 copy.59.refs_3_
  129.4 1.8 convolution_convert_fusion
  131.2 0.1 copy.58.refs_2_
  131.4 0.1 copy.57.refs_1_
  131.5 0.1 copy.60.refs_4_
  131.7 103.7 %scatter_blocks.1 = (f32[24,6272]{1,0:T(8,128)}, f32[96,768]{1,0:T(8,128)}) custom-call(bf16[128,768]{1,0:T(8,128)(2,1)S(1)} %copy-done, bf16[128,768]{1,0:T(8,128)(2,1)S(1)} %copy.57.refs_1_, bf16[128,768]{1,0:T(8,128)(2,1)S(1)} %copy.58.refs_2_, bf16[128,768]{1,0:T(8,128)(2,1)S(1)} %copy.59.refs_3_, bf16[128,768]{1,0:T(8,128)(2,1)S(1)} %copy.60.refs_4_, ...), custom_call_target="tpu_custom_call" | custom-call | tf_op jit(solution)/shard_map/scatter_blocks/pallas_call | solution.py:528
  235.4 1.2 broadcast_multiply_fusion
  236.6 0.7 fusion.61
  237.3 0.7 slice.145
  238.1 0.6 reshape.167
  238.7 0.8 slice_reduce_fusion
  239.5 0.7 broadcast_multiply_fusion.1
  240.3 1.8 convolution_add_fusion.2
  242.1 1.8 convolution_add_fusion.1
  243.9 2.6 %convolution_add_fusion = f32[128,768]{1,0:T(8,128)} fusion(f32[128,768]{1,0:T(8,128)S(1)} %convolution_add_fusion.1, bf16[128,768]{0,1:T(8,128)(2,1)S(1)} %bitcast.82, bf16[768,6272]{1,0:T(8,128)(2,1)} %bitcast.78), kind=kOutput, calls=%fused_computation.20 | convolution fusion | flops 151093248 | bytes 2162688 | tf_op jit(solution)/shard_map/dot_general | solution.py:187
  (43 shorter events, 0.5 us)
Async XLA Ops:
  87.5 3.0 %copy-start = (bf16[128,768]{1,0:T(8,128)(2,1)S(1)}, bf16[128,768]{1,0:T(8,128)(2,1)}, u32[]{:S(2)}) copy-start(bf16[128,768]{1,0:T(8,128)(2,1)} %refs_0_.3) | copy-start | bytes 589828
  90.6 2.9 %copy-start.6 = (bf16[768,128]{1,0:T(8,128)(2,1)}, bf16[768,128]{1,0:T(8,128)(2,1)S(1)}, u32[]{:S(2)}) copy-start(bf16[768,128]{1,0:T(8,128)(2,1)S(1)} %fusion.23) | copy-start | bytes 589828
  92.4 3.0 %copy-start.7 = (bf16[768,128]{1,0:T(8,128)(2,1)}, bf16[768,128]{1,0:T(8,128)(2,1)S(1)}, u32[]{:S(2)}) copy-start(bf16[768,128]{1,0:T(8,128)(2,1)S(1)} %convolution_convert_fusion.3) | copy-start | bytes 589828
  101.2 3.6 %copy-start.1 = (bf16[128,3072]{1,0:T(8,128)(2,1)}, bf16[128,3072]{1,0:T(8,128)(2,1)S(1)}, u32[]{:S(2)}) copy-start(bf16[128,3072]{1,0:T(8,128)(2,1)S(1)} %get-tuple-element.68.refs_8_) | copy-start | bytes 2359300
  101.2 5.6 %slice-start = ((s8[4718592]{0:T(1024)(128)(4,1)}), s8[4194304]{0:T(1024)(128)(4,1)S(1)}, s32[]{:S(2)}) async-start(s8[4718592]{0:T(1024)(128)(4,1)} %bitcast.65), calls=%async_computation | async-start | bytes 8388608
  101.2 3.8 %copy-start.2 = (f32[128,768]{1,0:T(8,128)S(1)}, f32[128,768]{1,0:T(8,128)}, u32[]{:S(2)}) copy-start(f32[128,768]{1,0:T(8,128)} %param.20) | copy-start | bytes 1179652
  101.2 5.6 %slice-start.1 = ((s8[4718592]{0:T(1024)(128)(4,1)}), s8[524288]{0:T(1024)(128)(4,1)S(1)}, s32[]{:S(2)}) async-start(s8[4718592]{0:T(1024)(128)(4,1)} %bitcast.65), calls=%async_computation.1 | async-start | bytes 1048576
  109.2 5.0 %copy-start.4 = (bf16[128,3072]{1,0:T(8,128)(2,1)}, bf16[128,3072]{1,0:T(8,128)(2,1)S(1)}, u32[]{:S(2)}) copy-start(bf16[128,3072]{1,0:T(8,128)(2,1)S(1)} %get-tuple-element.54.refs_7_) | copy-start | bytes 2359300
  118.4 9.9 %copy-start.3 = (f32[12,128,128]{1,2,0:T(8,128)}, f32[12,128,128]{1,2,0:T(8,128)S(1)}, u32[]{:S(2)}) copy-start(f32[12,128,128]{1,2,0:T(8,128)S(1)} %fusion.69) | copy-start | bytes 2359300
  118.4 1.9 copy-start.9
  124.5 0.6 copy-start.8
  235.4 4.1 %copy-start.5 = (f32[96,768]{1,0:T(8,128)S(1)}, f32[96,768]{1,0:T(8,128)}, u32[]{:S(2)}) copy-start(f32[96,768]{1,0:T(8,128)} %get-tuple-element.24) | copy-start | bytes 884740
